TPU v7x, 128 devices: a whole 4x4x4 slice. The times are simulated.
128 devices in a mesh: ctx: 8 (over y, x_hi), dp: 16 (over x_lo, z, core).
Axes of the slice: x: 4 (x_hi: 2, x_lo: 2; x = x_hi * 2 + x_lo), y: 4, z: 4, core: 2. Of those that a mesh axis runs over, the one named last changes fastest.
Arguments:
- events: bfloat16 [16, 4096, 512], P('dp', 'ctx'), may hold values from -6 to 6
- lengths: int32 [16, 4], P('dp'), may hold values from 1 to 3072, 4096 in all within a row
- target_rows: int32 [16, 1024], P('dp', 'ctx'), may hold values from 0 to 511, as said below
- position_ids: int32 [16, 1024], P('dp', 'ctx'), may hold values from 0 to 255
- labels: int32 [16, 1024], P('dp', 'ctx'), may hold values 0 or 1
- upstream: bfloat16 [16, 4096, 512], P('dp', 'ctx'), may hold values from -0.059814453 to 0.059814453
- w_in: bfloat16 [512, 2048], P(('ctx', 'dp')), may hold values from -0.25 to 0.25
- w_out: bfloat16 [512, 512], P(('ctx', 'dp')), may hold values from -0.25 to 0.25
- head_w1: bfloat16 [512, 256], replicated, may hold values from -0.25 to 0.25
- head_w2: float32 [256], replicated, may hold values from -0.375 to 0.375
- table: float32 [256, 128], replicated, may hold values from -6 to 6
- bias_w1: float32 [128, 128], replicated, may hold values from -0.5 to 0.5
- bias_w2: float32 [128], replicated, may hold values from -0.5 to 0.5
Outputs:
- grad_w_in: float32 [512, 2048], P(('ctx', 'dp'))
- grad_w_out: float32 [512, 512], P(('ctx', 'dp'))
- grad_head_w1: float32 [512, 256], P(('ctx', 'dp'))
- grad_head_w2: float32 [256], P(('ctx', 'dp'))
- grad_table: float32 [256, 128], P(('ctx', 'dp'))
- grad_bias_w1: float32 [128, 128], P(('ctx', 'dp'))
- grad_bias_w2: float32 [128], P(('ctx', 'dp'))
Inputs may be any that keep to these rules, and one draw needn't show every extreme that they name: Each group's 4 lengths sum to 4096. `target_rows`: the 128 entries of one device are distinct.
All inputs are finite; a program needn't handle non-finite values. No bound on the sum of `labels` on one device may be relied on, other than what follows from the above.
Results may differ from a plain program's by a relative error of at most 0.0095.
Values may be sent and summed in bfloat16 or wider, within the bound.
No kernel may reach another device: no remote copies, remote signals or barrier semaphores. Data moves between devices by JAX's collectives and lax.ppermute only.
A program may use at most 192 MiB of HBM per device.

v0:
```python
import functools
import math

import jax
import jax.numpy as jnp
from jax import lax
from jax.experimental import pallas as pl
from jax.experimental.pallas import tpu as pltpu
from jax.sharding import Mesh, PartitionSpec as P

HEADS = 4
EPSILON = 1e-05
HIGHEST = lax.Precision.HIGHEST
F32 = jnp.float32
BF16 = jnp.bfloat16
I32 = jnp.int32
R = 512
W = 512
E = 128
T = 128
SCALE = 1.0 / math.sqrt(E)
HALF = 0.5 * SCALE

NN = (((1,), (0,)), ((), ()))
NT = (((1,), (1,)), ((), ()))
TN = (((0,), (0,)), ((), ()))


def mm(a, b, dims=NN, precision=None):
    return lax.dot_general(a, b, dims, precision=precision, preferred_element_type=F32)


def silu_parts(z):
    h = 0.5 * z
    t = jnp.tanh(h)
    a = 1.0 + t
    w = h * a
    return w, 0.5 * (a + w * (1.0 - t))


def silu(z):
    h = 0.5 * z
    return h + h * jnp.tanh(h)


def vmem(n):
    return [pl.BlockSpec(memory_space=pltpu.VMEM)] * n


def smem():
    return [pl.BlockSpec(memory_space=pltpu.SMEM)]


def call(kernel, outs, args, scratch=(), limit=24, flops=0, n_smem=1, n_any=0, name=None):
    total = sum(a.size * a.dtype.itemsize for a in args) + sum(
        math.prod(o.shape) * o.dtype.itemsize for o in outs
    )
    return pl.pallas_call(
        kernel,
        out_shape=tuple(outs),
        in_specs=smem() * n_smem
        + vmem(len(args) - n_smem - n_any)
        + [pl.BlockSpec(memory_space=pl.ANY)] * n_any,
        out_specs=tuple(vmem(len(outs))),
        scratch_shapes=list(scratch),
        compiler_params=pltpu.CompilerParams(vmem_limit_bytes=limit << 20),
        cost_estimate=pl.CostEstimate(flops=flops, bytes_accessed=total, transcendentals=0),
        name=name,
    )(*args)


def sds(shape, dtype):
    return jax.ShapeDtypeStruct(shape, dtype)


def plane_kernel(coords, q0, q1, q2, q3, out):
    for k, ref in enumerate((q0, q1, q2, q3)):
        out[pl.ds(pl.multiple_of(((coords[1] + 4 - k) & 3) * 32, 32), 32), :] = ref[...]


def cube_kernel(coords, q0, q1, q2, q3, out, half, rows):
    for k, ref in enumerate((q0, q1, q2, q3)):
        z = ((coords[2] + 4 - k) & 3) * 8
        part = ref[...].astype(F32)
        for i in range(4):
            for j in range(4):
                at = i * 32 + j * 8
                rows[pl.ds(pl.multiple_of(j * E + i * 32 + z, 8), 8), :] = part[at : at + 8]
    out[...] = rows[:, : 3 * E].astype(BF16)
    half[...] = rows[:, 3 * E :].astype(BF16)


def norm_kernel(x_ref, _, o_ref):
    x = x_ref[...].astype(F32)
    mean = jnp.mean(x, axis=-1, keepdims=True)
    cen = x - mean
    inv = lax.rsqrt(jnp.mean(cen * cen, axis=-1, keepdims=True) + EPSILON)
    o_ref[...] = (cen * inv).astype(BF16)


def user_start(pos, meta):
    start = jnp.zeros_like(pos)
    end = 0
    for j in range(3):
        end = end + meta[3, 2 + j]
        start = jnp.where(pos >= end, end, start)
    return start


def places(y, core):
    s = jnp.where(core == 0, 3, 1)
    back, on, far = (y + s) & 3, (y + 4 - s) & 3, (y + 2) & 3
    return (y, back, on, far), (y, on, back, far)


def key_range(base, rows, meta):
    lo = user_start(base, meta)
    last = base + rows - 1
    end = last // R + 1
    first = lo // R
    diag = base // R
    full = jnp.clip((user_start(last, meta) + R - 1) // R, first, diag)
    return first, full, diag, end


def forward_kernel(meta, n0, na, nb, nc, o0, oa, ob, oc, wg, a0, a1, a2, a3, q_s, k_s, v_s, sent):
    y, core = meta[3, 0], meta[3, 1]
    own, oth = places(y, core)
    for blk, ref in zip(own, (n0, na, nb, nc)):
        b = 2 * blk + core
        p = silu(mm(ref[...], wg[:, : 3 * E])).astype(BF16)
        q_s[blk] = p[:, :E]
        k_s[b] = p[:, E : 2 * E]
        v_s[b] = p[:, 2 * E :]
    for blk, ref in zip(oth, (o0, oa, ob, oc)):
        b = 2 * blk + 1 - core
        p = silu(mm(ref[...], wg[:, E : 3 * E])).astype(BF16)
        k_s[b] = p[:, :E]
        v_s[b] = p[:, E:]
    rows = lax.broadcasted_iota(I32, (R, 1), 0)
    lanes = lax.broadcasted_iota(I32, (1, R), 1)

    def block(k, _):
        blk = (y + k) & 3
        c = 2 * blk + core
        q = q_s[blk]
        pos = rows + c * R
        start = user_start(pos, meta)

        def step(b, acc, masked):
            h = mm(q, k_s[b], NT) * HALF
            w = h + h * jnp.tanh(h)
            if masked:
                key_pos = lanes + b * R
                w = jnp.where((key_pos >= start) & (key_pos <= pos), w, 0.0)
            return acc + mm(w.astype(BF16), v_s[b])

        first, full, diag, end = key_range(c * R, R, meta)
        acc = jnp.zeros((R, E), F32)
        acc = lax.fori_loop(first, full, functools.partial(step, masked=True), acc)
        acc = lax.fori_loop(full, diag, functools.partial(step, masked=False), acc)
        acc = lax.fori_loop(diag, end, functools.partial(step, masked=True), acc)
        mean = jnp.mean(acc, axis=-1, keepdims=True).astype(BF16)
        sent[k, :R] = (acc - mean.astype(F32)).astype(BF16)
        one = (lax.broadcasted_iota(I32, (16, E), 1) == 0).astype(BF16)
        line = mm(one, jnp.broadcast_to(mean, (R, E)), NT)
        sent[k, R:] = jnp.concatenate(
            [line[0:1, i * E : (i + 1) * E] for i in range(4)] + [jnp.zeros((12, E), F32)], axis=0
        ).astype(BF16)
        return 0

    lax.fori_loop(0, 4, block, 0)
    for k, out in enumerate((a0, a1, a2, a3)):
        out[...] = sent[k]


def side_kernel(
    meta, n0, w_mine, wo_half, events, ints, table, bias_w1, bias_w2, u, su, w_out, ev_t, emb, bpre, obs
):
    first = meta[3, 1] == 0
    mine = w_mine[...]
    other = wo_half[...]
    w_u = jnp.where(first, mine, other)
    w_out[...] = jnp.where(first, other, mine)
    act, slope = silu_parts(mm(n0[...], w_u))
    u[...] = act.astype(BF16)
    su[...] = slope.astype(BF16)
    placing = (lax.broadcasted_iota(I32, (R, T), 0) == ints[0:1, :]).astype(BF16)
    ev_t[...] = mm(placing, events[...], TN)
    pid = jnp.broadcast_to(ints[1:2, :], (T, T)).astype(F32).T.astype(I32)
    pid = jnp.concatenate([pid, pid], axis=1)
    selector = (lax.broadcasted_iota(I32, (T, 2 * T), 1) == pid).astype(F32)
    embedded = mm(selector, table[...], precision=HIGHEST)
    bias_pre = mm(embedded, bias_w1[...], precision=HIGHEST)
    emb[...] = embedded
    bpre[...] = bias_pre
    hid = silu(bias_pre)
    obs[...] = jnp.broadcast_to(jnp.sum(hid * bias_w2[...], axis=1, keepdims=True), (T, E))


def slopes_kernel(meta, n0, na, nb, nc, wg, _, s_o, nt, kt):
    y, core = meta[3, 0], meta[3, 1]
    width = s_o.shape[2]
    own, oth = places(y, core)
    for blk, ref in zip(own if width == 3 * E else oth, (n0, na, nb, nc)):
        x = ref[...]
        act, slope = silu_parts(mm(x, wg[:, 3 * E - width : 3 * E]))
        s_o[blk] = slope.astype(BF16)
        kt[blk] = act[:, width - 2 * E : width - E].astype(BF16).T
        nt[blk] = x.T


def middle_kernel(
    meta, r0, r1, r2, r3, u, su, w_out, ev_t, obs, ints, upstream, head_w1, head_w2,
    d0, d1, d2, d3, gated_o, dout_o, dpre_o, picked_o, dhid_o, act_o, drel_o, dobs_o,
    att,
):
    y = meta[3, 0]
    for k, ref in enumerate((r0, r1, r2, r3)):
        h = (y + 4 - k) & 3
        means = ref[R:]
        pick = lax.broadcasted_iota(I32, (16, E), 0)
        column = jnp.concatenate([mm(means, (pick == i).astype(BF16), TN) for i in range(4)], axis=0)
        att[:, pl.ds(pl.multiple_of(h * E, E), E)] = ref[:R].astype(F32) + column
    x = att[...]
    mean = jnp.mean(x, axis=-1, keepdims=True)
    cen = x - mean
    inv = lax.rsqrt(jnp.mean(cen * cen, axis=-1, keepdims=True) + EPSILON)
    normed = cen * inv
    gate = u[...].astype(F32)
    gated = (normed * gate).astype(BF16)
    gated_o[...] = gated
    placing = (lax.broadcasted_iota(I32, (R, T), 0) == ints[0:1, :]).astype(BF16)
    gated_t = mm(placing, gated, TN).astype(BF16)
    picked = (mm(gated_t, w_out[...]) + ev_t[...]).astype(BF16)
    picked_o[...] = picked
    hidden = mm(picked, head_w1[...])
    active, slope = silu_parts(hidden)
    act_o[...] = active
    w2 = head_w2[...]
    relevance = jnp.sum(active * w2, axis=1, keepdims=True)
    observe = obs[:, :1]
    clicked = jnp.broadcast_to(ints[2:3, :], (T, T)).astype(F32).T[:, :1]
    rel_sig = jax.nn.sigmoid(relevance)
    obs_sig = jax.nn.sigmoid(observe)
    missing = jax.nn.sigmoid(-relevance) + rel_sig * jax.nn.sigmoid(-observe)
    d_rel = clicked * (rel_sig - 1.0) + (1.0 - clicked) * rel_sig * (1.0 - rel_sig) * obs_sig / missing
    d_obs = clicked * (obs_sig - 1.0) + (1.0 - clicked) * rel_sig * obs_sig * (1.0 - obs_sig) / missing
    drel_o[...] = jnp.broadcast_to(d_rel, (T, E))
    dobs_o[...] = jnp.broadcast_to(d_obs, (T, E))
    d_hidden = (d_rel * w2 * slope).astype(BF16)
    dhid_o[...] = d_hidden
    d_picked = mm(d_hidden, head_w1[...], NT).astype(BF16)
    d_out = (upstream[...].astype(F32) + mm(placing, d_picked)).astype(BF16)
    dout_o[...] = d_out
    d_gated = mm(d_out, w_out[...], NT)
    dpre_o[...] = (d_gated * normed * su[...].astype(F32)).astype(BF16)
    g = d_gated * gate
    first = jnp.mean(g, axis=-1, keepdims=True)
    second = jnp.mean(g * normed, axis=-1, keepdims=True)
    att[...] = inv * (g - first - normed * second)
    for k, ref in enumerate((d0, d1, d2, d3)):
        h = (y + k) & 3
        ref[...] = att[:, pl.ds(pl.multiple_of(h * E, E), E)].astype(BF16)


def packed(left, right):
    low = (lax.broadcasted_iota(I32, left.shape, 0) & 7) < 4
    n = left.shape[0]
    return jnp.where(low, left, pltpu.roll(right, 4, 0)), jnp.where(low, pltpu.roll(left, n - 4, 0), right)


def grads_kernel(
    meta, n0, dpre, gated, d_out, picked, d_hid, active, d_rel, d_obs, ints, emb, bpre, bias_w1, bias_w2,
    x_own, x_oth, s_own, s_oth,
):
    first = meta[3, 1] == 0

    def put(own_ref, oth_ref, col, left, right):
        x_0, x_1 = packed(left, right)
        cols = slice(col, col + left.shape[1])
        own_ref[:, cols] = jnp.where(first, x_0, x_1).astype(BF16)
        oth_ref[:, cols] = jnp.where(first, x_1, x_0).astype(BF16)

    g_u = mm(n0[...], dpre[...], TN)
    put(x_own, x_oth, 0, g_u[:, :256], g_u[:, 256:])
    g_wo = mm(gated[...], d_out[...], TN)
    put(x_own, x_oth, 256, g_wo[:, :256], g_wo[:, 256:])
    g_h1 = mm(picked[...], d_hid[...], TN)
    put(x_own, x_oth, 512, g_h1[:, :128], g_h1[:, 128:])
    hid, slope = silu_parts(bpre[...])
    d_bias = d_obs[...] * bias_w2[...] * slope
    g_b1 = mm(emb[...], d_bias, TN, HIGHEST)
    d_emb = mm(d_bias, bias_w1[...], NT, HIGHEST)
    pid = jnp.broadcast_to(ints[1:2, :], (2 * T, T))
    select_t = (lax.broadcasted_iota(I32, (2 * T, T), 0) == pid).astype(F32)
    g_tab = mm(select_t, d_emb, precision=HIGHEST)
    h2 = mm(active[...], d_rel[...], TN, HIGHEST)
    b2 = mm(hid, d_obs[...], TN, HIGHEST)
    lane2 = lax.broadcasted_iota(I32, (2 * T, E), 1)
    row2 = lax.broadcasted_iota(I32, (2 * T, E), 0)
    h2 = jnp.where(lane2 == (row2 & 1), h2, 0.0)
    b2 = jnp.where(lax.broadcasted_iota(I32, (T, E), 1) == 2, b2, 0.0)
    o2 = lax.broadcasted_iota(I32, (R, 2 * T), 0)
    i2 = lax.broadcasted_iota(I32, (R, 2 * T), 1)
    o1 = lax.broadcasted_iota(I32, (R, T), 0)
    i1 = lax.broadcasted_iota(I32, (R, T), 1)
    parts = []
    for cc in range(2):
        dest2 = 2 * (o2 >> 3) + cc
        dest1 = 2 * (o1 >> 3) + cc
        p_tab = (((o2 & 7) == 4) & (i2 == 2 * dest2)) | (((o2 & 7) == 5) & (i2 == 2 * dest2 + 1))
        p_h2 = ((o2 & 7) == 7) & ((i2 >> 1) == dest2)
        p_b1 = ((o1 & 7) == 6) & (i1 == dest1)
        p_b2 = ((o1 & 7) == 7) & (i1 == dest1)
        parts.append(
            mm(p_tab.astype(BF16), g_tab.astype(BF16))
            + mm(p_h2.astype(BF16), h2.astype(BF16))
            + mm(p_b1.astype(BF16), g_b1.astype(BF16))
            + mm(p_b2.astype(BF16), b2.astype(BF16))
        )
    s_own[...] = jnp.where(first, parts[0], parts[1]).astype(BF16)
    s_oth[...] = jnp.where(first, parts[1], parts[0]).astype(BF16)


def backward_kernel(
    meta, q_s, k_s, v_s, r0, r1, r2, r3, s_a, s_b, nt_a, nt_b, kt_a, kt_b, s_own, s_oth,
    x_own, x_oth,
    dq_s, dk_s, dv_s, kt_s, g_s,
):
    y, core = meta[3, 0], meta[3, 1]
    for i in range(4):
        kt_s[2 * i + core] = kt_a[i]
        kt_s[2 * i + 1 - core] = kt_b[i]
    dk_s[...] = jnp.zeros_like(dk_s)
    dv_s[...] = jnp.zeros_like(dv_s)
    rows = lax.broadcasted_iota(I32, (R, 1), 0)
    lanes = lax.broadcasted_iota(I32, (1, R), 1)
    for k, ref in enumerate((r0, r1, r2, r3)):
        g_s[(y + 4 - k) & 3] = ref[...]

    def block(blk, _):
        c = 2 * blk + core
        q = q_s[blk]
        g = g_s[blk]
        pos = lanes + c * R
        start = user_start(pos, meta)

        def step(b, dq, masked):
            kb = k_s[b]
            h = mm(kb, q, NT) * HALF
            dp = mm(v_s[b], g, NT)
            t = jnp.tanh(h)
            a = 1.0 + t
            w = h * a
            d = dp * (a + w * (1.0 - t))
            if masked:
                key_pos = rows + b * R
                keep = (key_pos >= start) & (key_pos <= pos)
                w = jnp.where(keep, w, 0.0)
                d = jnp.where(keep, d, 0.0)
            w = w.astype(BF16)
            d = d.astype(BF16)
            dv_s[b] += mm(w, g)
            dk_s[b] += mm(d, q)
            return dq + mm(kt_s[b], d)

        first, full, diag, end = key_range(c * R, R, meta)
        acc = jnp.zeros((E, R), F32)
        acc = lax.fori_loop(first, full, functools.partial(step, masked=True), acc)
        acc = lax.fori_loop(full, diag, functools.partial(step, masked=False), acc)
        acc = lax.fori_loop(diag, end, functools.partial(step, masked=True), acc)
        dq_s[blk] = acc.T
        return 0

    lax.fori_loop(0, 4, block, 0)
    g_all = jnp.zeros((W, 3 * E), F32)
    g_kv = jnp.zeros((W, 2 * E), F32)
    for i in range(4):
        b = 2 * i + core
        d = jnp.concatenate([dq_s[i] * HALF, dk_s[b] * HALF, dv_s[b]], axis=1) * s_a[i].astype(F32)
        g_all = g_all + mm(nt_a[i], d.astype(BF16))
        b = 2 * i + 1 - core
        d = jnp.concatenate([dk_s[b] * HALF, dv_s[b]], axis=1) * s_b[i].astype(F32)
        g_kv = g_kv + mm(nt_b[i], d.astype(BF16))
    g_q = g_all[:, :E]
    g_k = g_all[:, E : 2 * E] + g_kv[:, :E]
    g_v = g_all[:, 2 * E :] + g_kv[:, E:]
    first = core == 0
    low = (lax.broadcasted_iota(I32, (W, E), 0) & 7) < 4
    x_0, x_1 = packed(g_q, g_k)
    x_own[:, :E] = jnp.where(first, x_0, x_1).astype(BF16)
    x_oth[:, :E] = jnp.where(first, x_1, x_0).astype(BF16)
    v_1 = pltpu.roll(g_v, W - 4, 0)
    x_own[:, E:] = jnp.where(low, jnp.where(first, g_v, v_1), s_own[...].astype(F32)).astype(BF16)
    x_oth[:, E:] = jnp.where(low, jnp.where(first, v_1, g_v), s_oth[...].astype(F32)).astype(BF16)


def sum_kernel(x_ref, g_in, g_out, g_h1, g_h2, g_tab, g_b1, g_b2):
    total = None
    for h in range(HEADS):
        part = jnp.zeros((8, 7 * E), F32)
        for i in range(16):
            at = (h * 16 + i) * 8
            part = part + x_ref[at : at + 8, :].astype(F32)
        g_in[:, W + h * E : W + (h + 1) * E] = part[0:4, 6 * E :]
        g_in[:, 2 * W + h * E : 2 * W + (h + 1) * E] = part[0:4, 5 * E : 6 * E]
        g_in[:, 3 * W + h * E : 3 * W + (h + 1) * E] = part[4:8, 5 * E : 6 * E]
        total = part if total is None else total + part
    g_in[:, 0:256] = total[0:4, 0:256]
    g_in[:, 256:512] = total[4:8, 0:256]
    g_out[:, 0:256] = total[0:4, 256:512]
    g_out[:, 256:512] = total[4:8, 256:512]
    g_h1[:, 0:128] = total[0:4, 512:640]
    g_h1[:, 128:256] = total[4:8, 512:640]
    g_tab[...] = total[4:6, 768:896]
    g_b1[...] = total[6:7, 768:896]
    g_h2[...] = total[7:8, 768:770]
    g_b2[...] = total[7:8, 770:771]


CHIPS = ("y", "xh", "xl", "z")
SWAP = []
for _i in range(32):
    _xh, _rest, _core = _i // 16, (_i // 2) % 8, _i % 2
    SWAP.append((_i, _i if _xh == _core else (1 - _xh) * 16 + _rest * 2 + 1 - _core))


def swapped(x):
    return lax.ppermute(x, ("xh", "xl", "z", "core"), SWAP)


def across(x):
    return lax.ppermute(x, "core", [(0, 1), (1, 0)])


def ring(x, k):
    return lax.ppermute(x, "y", [(i, (i + k) % 4) for i in range(4)])


def moved(x, axes, k):
    return lax.ppermute(x, axes, [(i, (i + k) % 4) for i in range(4)])


def tie(x, other):
    space = pl.BlockSpec(memory_space=pltpu.VMEM)
    return pl.pallas_call(
        lambda *_: None,
        out_shape=sds(x.shape, x.dtype),
        in_specs=[space] * 2,
        out_specs=space,
        compiler_params=pltpu.CompilerParams(vmem_limit_bytes=4 << 20),
        input_output_aliases={0: 0},
        name="tie",
    )(x, other)


def turned(x, k):
    return lax.ppermute(
        x, ("y", "core"), [(2 * i + c, 2 * ((i + (k if c == 0 else -k)) % 4) + c) for i in range(4) for c in range(2)]
    )


def body(
    events, lengths, target_rows, position_ids, labels, upstream,
    w_in, w_out, head_w1, head_w2, table, bias_w1, bias_w2,
):
    y, core = lax.axis_index("y"), lax.axis_index("core")
    w_rows = jnp.concatenate([w_in, w_out], axis=1)
    w_other = across(w_rows)
    w_rows = jnp.where(
        core == 0, jnp.concatenate([w_rows, w_other], axis=0), jnp.concatenate([w_other, w_rows], axis=0)
    )
    shared = jnp.where(core == 0, w_rows[:, :W], w_rows[:, 4 * W :])
    w_rows = jnp.concatenate([w_rows[:, W : 4 * W], shared], axis=1)
    x, z = 2 * lax.axis_index("xh") + lax.axis_index("xl"), lax.axis_index("z")
    line = [moved(w_rows, ("y",), k) for k in (3, 2, 1)]
    line = jnp.concatenate(line + [w_rows] + line, axis=0)
    line = lax.dynamic_slice_in_dim(line, ((3 - y) & 3) * 8, 32, 0)
    line = jnp.concatenate(
        [lax.dynamic_slice_in_dim(line, at + y * E, E, 1) for at in (W, 2 * W, 0)] + [line[:, 3 * W :]], axis=1
    )
    coords = jnp.stack([y, x, z]).astype(I32)
    (plane,) = call(
        plane_kernel,
        [sds((E, 7 * E), BF16)],
        [coords, line] + [moved(line, ("xh", "xl"), k) for k in (1, 2, 3)],
        limit=8,
        name="plane",
    )
    wg, w_mine = call(
        cube_kernel,
        [sds((W, 3 * E), BF16), sds((W, W), BF16)],
        [coords, plane] + [moved(plane, ("z",), k) for k in (1, 2, 3)],
        scratch=[pltpu.VMEM((W, 7 * E), F32)],
        limit=12,
        name="cube",
    )

    w_half = across(w_mine)

    ev = swapped(events[0])
    place = jnp.stack([y, lax.axis_index("xh")]).astype(I32)[None]
    line = jnp.pad(jnp.concatenate([place, lengths], axis=1), ((0, 0), (0, T - 6)))
    ints = swapped(jnp.concatenate([target_rows, position_ids, labels, line], axis=0))
    meta = ints
    (n0,) = call(norm_kernel, [sds((R, W), BF16)], [ev, line], n_smem=0, n_any=1, limit=12, name="norm")
    na = turned(n0, 1)
    nb = turned(n0, 3)
    na = tie(na, plane)
    nc = turned(na, 1)
    n0, nb, na = tie(n0, wg), tie(nb, wg), tie(na, nc)
    parts = [n0, na, nb, nc]
    parts = parts + [across(p) for p in parts]
    up = swapped(upstream[0])

    qkv = [sds((4, R, E), BF16), sds((8, R, E), BF16), sds((8, R, E), BF16)]
    a0, a1, a2, a3, q_s, k_s, v_s = call(
        forward_kernel, [sds((R + 16, E), BF16)] * 4 + qkv, [meta] + parts + [wg], flops=5 * 10**9,
        scratch=[pltpu.VMEM((4, R + 16, E), BF16)], name="forward",
    )
    r1, r2, r3 = ring(a1, 1), ring(a2, 2), ring(a3, 3)
    u, su, w_o, ev_t, emb, bpre, obs = call(
        side_kernel,
        [sds((R, W), BF16)] * 3 + [sds((T, W), F32)] + [sds((T, E), F32)] * 3,
        [meta, n0, w_mine, w_half, ev, ints, table, bias_w1, bias_w2.reshape(1, E)],
        flops=10**9,
        name="side",
    )

    def slopes(width, blocks, after):
        return call(
            slopes_kernel,
            [sds((4, R, width), BF16), sds((4, W, R), BF16), sds((4, E, R), BF16)],
            [meta] + blocks + [wg, after],
            n_any=1,
            flops=10**9,
            name="slopes",
        )

    s_a, nt_a, kt_a = slopes(3 * E, parts[:4], a0)
    w2 = head_w2.reshape(1, 2 * E)
    b2 = bias_w2.reshape(1, E)
    d0, d1, d2, d3, gated, d_out, dpre, picked, d_hid, active, d_rel, d_obs = call(
        middle_kernel,
        [sds((R, E), BF16)] * 4
        + [sds((R, W), BF16)] * 3
        + [sds((T, W), BF16), sds((T, 2 * E), BF16), sds((T, 2 * E), F32), sds((T, E), F32), sds((T, E), F32)],
        [meta, a0, r1, r2, r3, u, su, w_o, ev_t, obs, ints, up, head_w1, w2],
        scratch=[pltpu.VMEM((R, W), F32)],
        flops=10**9,
        name="middle",
    )
    g1, g2, g3 = ring(d1, 1), ring(d2, 2), ring(d3, 3)
    s_b, nt_b, kt_b = slopes(2 * E, parts[4:], d0)
    early, early_oth, s_own, s_oth = call(
        grads_kernel,
        [sds((R, 5 * E), BF16)] * 2 + [sds((R, E), BF16)] * 2,
        [meta, n0, dpre, gated, d_out, picked, d_hid, active, d_rel, d_obs, ints, emb, bpre, bias_w1, b2],
        flops=2 * 10**9,
        name="grads",
    )
    early_in = across(early_oth)
    late, late_oth = call(
        backward_kernel,
        [sds((R, 2 * E), BF16)] * 2,
        [meta, q_s, k_s, v_s, d0, g1, g2, g3, s_a, s_b, nt_a, nt_b, kt_a, kt_b, s_own, s_oth],
        scratch=[pltpu.VMEM((4, R, E), F32), pltpu.VMEM((8, R, E), F32), pltpu.VMEM((8, R, E), F32)]
        + [pltpu.VMEM((8, E, R), BF16), pltpu.VMEM((4, R, E), BF16)],
        flops=10**10,
        limit=28,
        name="backward",
    )
    late_in = across(late_oth)
    pair = jnp.concatenate(
        [
            (early.astype(F32) + early_in.astype(F32)).astype(BF16),
            (late.astype(F32) + late_in.astype(F32)).astype(BF16),
        ],
        axis=1,
    )
    got = lax.all_to_all(pair, CHIPS, 0, 0, tiled=True)
    g_in, g_out, g_h1, g_h2, g_tab, g_b1, g_b2 = call(
        sum_kernel,
        [sds((4, 4 * W), F32), sds((4, W), F32), sds((4, 2 * E), F32)]
        + [sds((1, 2), F32), sds((2, E), F32), sds((1, E), F32), sds((1, 1), F32)],
        [got],
        n_smem=0,
        name="total",
    )
    return g_in, g_out, g_h1, g_h2.reshape(2), g_tab, g_b1, g_b2.reshape(1)


def solution(mesh):
    fine = Mesh(mesh.devices.reshape(4, 2, 2, 4, 2), ("y", "xh", "xl", "z", "core"))
    ctx, dp = ("y", "xh"), ("xl", "z", "core")
    every = ctx + dp
    in_specs = (
        P(dp, ctx, None),
        P(dp, None),
        P(dp, ctx),
        P(dp, ctx),
        P(dp, ctx),
        P(dp, ctx, None),
        P(every, None),
        P(every, None),
        P(),
        P(),
        P(),
        P(),
        P(),
    )
    out_specs = (
        P(every, None),
        P(every, None),
        P(every, None),
        P(every),
        P(every, None),
        P(every, None),
        P(every),
    )
    return jax.shard_map(body, mesh=fine, in_specs=in_specs, out_specs=out_specs, check_vma=False)
```

profile of v0, /device:TPU:0, one launch (start us, length us, event | category | flops | bytes accessed | tf_op | source)
XLA Modules:
  0.0 139.4 jit_solution(4304804239795880544)
XLA Ops:
  2.1 1.7 %collective-permute-start.1 = (bf16[512,512]{1,0:T(8,128)(2,1)}, bf16[512,512]{1,0:T(8,128)(2,1)S(1)}, u32[]{:S(2)}, u32[]{:S(2)}) collective-permute-start(bf16[512,512]{1,0:T(8,128)(2,1)} %bitcast.19), channel_id=1, source_target_pairs={{0,0},{1,16},{2,2},{3,18},{4,4},{5,20},{6,6},{7,22},{8,8},{9,24},{... | collective-permute-start | bytes 1572872 | tf_op jit(solution)/shard_map/ppermute | solution.py:430
  3.9 3.2 %collective-permute-start.3 = (bf16[8,2048]{1,0:T(8,128)(2,1)S(1)}, bf16[8,2048]{1,0:T(8,128)(2,1)S(1)}, u32[]{:S(2)}, u32[]{:S(2)}) collective-permute-start(bf16[8,2048]{1,0:T(8,128)(2,1)S(1)} %pad_maximum_fusion.1), channel_id=1, source_target_pairs={{0,96},{32,0},{64,32},{96,64},{1,97},{33,1},{65,33},{97,65},{2,98}... | collective-permute-start | bytes 98312 | tf_op jit(solution)/shard_map/ppermute | solution.py:442
  7.8 2.2 %collective-permute-start.4 = (bf16[8,2048]{1,0:T(8,128)(2,1)S(1)}, bf16[8,2048]{1,0:T(8,128)(2,1)S(1)}, u32[]{:S(2)}, u32[]{:S(2)}) collective-permute-start(bf16[8,2048]{1,0:T(8,128)(2,1)S(1)} %pad_maximum_fusion.1), channel_id=1, source_target_pairs={{0,64},{32,96},{64,0},{96,32},{1,65},{33,97},{65,1},{97,33},{2,66}... | collective-permute-start | bytes 98312 | tf_op jit(solution)/shard_map/ppermute | solution.py:442
  10.0 3.3 %collective-permute-done.4 = bf16[8,2048]{1,0:T(8,128)(2,1)S(1)} collective-permute-done((bf16[8,2048]{1,0:T(8,128)(2,1)S(1)}, bf16[8,2048]{1,0:T(8,128)(2,1)S(1)}, u32[]{:S(2)}, u32[]{:S(2)}) %collective-permute-start.4) | collective-permute-done | bytes 32800 | tf_op jit(solution)/shard_map/ppermute | solution.py:442
  14.4 4.9 %collective-permute-start.8 = (bf16[32,896]{1,0:T(8,128)(2,1)S(1)}, bf16[32,896]{1,0:T(8,128)(2,1)S(1)}, u32[]{:S(2)}, u32[]{:S(2)}) collective-permute-start(bf16[32,896]{1,0:T(8,128)(2,1)S(1)} %pad_maximum_fusion.q0), channel_id=1, source_target_pairs={{0,24},{8,0},{16,8},{24,16},{1,25},{9,1},{17,9},{25,17},{2,26},{10... | collective-permute-start | bytes 172040 | tf_op jit(solution)/shard_map/ppermute | solution.py:442
  19.6 1.3 collective-permute-start.6
  21.0 1.7 %collective-permute-start.14 = (bf16[512,512]{1,0:T(8,128)(2,1)S(1)}, bf16[512,512]{1,0:T(8,128)(2,1)S(1)}, u32[]{:S(2)}, u32[]{:S(2)}) collective-permute-start(bf16[512,512]{1,0:T(8,128)(2,1)S(1)} %norm.1.__0_), channel_id=1, source_target_pairs={{0,96},{1,33},{32,0},{33,65},{64,32},{65,97},{96,64},{97,1},{2,98}... | collective-permute-start | bytes 1572872 | tf_op jit(solution)/shard_map/ppermute | solution.py:459
  22.8 2.5 %collective-permute-done.7.q2 = bf16[32,896]{1,0:T(8,128)(2,1)S(1)} collective-permute-done((bf16[32,896]{1,0:T(8,128)(2,1)S(1)}, bf16[32,896]{1,0:T(8,128)(2,1)S(1)}, u32[]{:S(2)}, u32[]{:S(2)}) %collective-permute-start.7) | collective-permute-done | bytes 57376 | tf_op jit(solution)/shard_map/ppermute | solution.py:442
  25.2 0.8 collective-permute-done.6.q1
  26.6 1.2 collective-permute-start.13
  27.8 4.0 %collective-permute-start.11 = (bf16[128,896]{1,0:T(8,128)(2,1)S(1)}, bf16[128,896]{1,0:T(8,128)(2,1)S(1)}, u32[]{:S(2)}, u32[]{:S(2)}) collective-permute-start(bf16[128,896]{1,0:T(8,128)(2,1)S(1)} %plane.1.q0.__1_), channel_id=1, source_target_pairs={{0,6},{2,0},{4,2},{6,4},{1,7},{3,1},{5,3},{7,5},{8,14},{10,8},{12,... | collective-permute-start | bytes 688136 | tf_op jit(solution)/shard_map/ppermute | solution.py:442
  31.9 1.3 collective-permute-start.9
  33.1 9.1 %collective-permute-done.11.q3 = bf16[128,896]{1,0:T(8,128)(2,1)S(1)} collective-permute-done((bf16[128,896]{1,0:T(8,128)(2,1)S(1)}, bf16[128,896]{1,0:T(8,128)(2,1)S(1)}, u32[]{:S(2)}, u32[]{:S(2)}) %collective-permute-start.11) | collective-permute-done | bytes 229408 | tf_op jit(solution)/shard_map/ppermute | solution.py:442
  42.2 3.4 %collective-permute-done.9.q1 = bf16[128,896]{1,0:T(8,128)(2,1)S(1)} collective-permute-done((bf16[128,896]{1,0:T(8,128)(2,1)S(1)}, bf16[128,896]{1,0:T(8,128)(2,1)S(1)}, u32[]{:S(2)}, u32[]{:S(2)}) %collective-permute-start.9) | collective-permute-done | bytes 229408 | tf_op jit(solution)/shard_map/ppermute | solution.py:442
  45.7 0.8 cube.1
  48.3 5.8 %collective-permute-start.22 = (bf16[512,512]{1,0:T(8,128)(2,1)S(1)}, bf16[512,512]{1,0:T(8,128)(2,1)S(1)}, u32[]{:S(2)}, u32[]{:S(2)}) collective-permute-start(bf16[512,512]{1,0:T(8,128)(2,1)S(1)} %get-tuple-element.59.w_mine), channel_id=1, source_target_pairs={{0,1},{1,0},{2,3},{3,2},{4,5},{5,4},{6,7},{7,6},{8,9},{9,8},{10,11... | collective-permute-start | bytes 1572872 | tf_op jit(solution)/shard_map/ppermute | solution.py:434
  54.2 0.8 collective-permute-start.23
  55.1 10.0 %forward.1 = (bf16[528,128]{1,0:T(8,128)(2,1)S(1)}, bf16[528,128]{1,0:T(8,128)(2,1)S(1)}, bf16[528,128]{1,0:T(8,128)(2,1)S(1)}, bf16[528,128]{1,0:T(8,128)(2,1)S...) custom-call(s32[4,128]{1,0:T(4,128)S(1)} %collective-permute-done.meta.int, ...), custom_call_target="tpu_custom_call" | custom-call | flops 5000000000 | bytes 7751680 | tf_op jit(solution)/shard_map/forward/pallas_call | solution.py:58
  65.5 1.4 %collective-permute-start.20 = (bf16[528,128]{1,0:T(8,128)(2,1)S(1)}, bf16[528,128]{1,0:T(8,128)(2,1)S(1)}, u32[]{:S(2)}, u32[]{:S(2)}) collective-permute-start(bf16[528,128]{1,0:T(8,128)(2,1)S(1)} %get-tuple-element.57), channel_id=1, source_target_pairs={{0,64},{32,96},{64,0},{96,32},{1,65},{33,97},{65,1},{97,33},{2,66}... | collective-permute-start | bytes 405512 | tf_op jit(solution)/shard_map/ppermute | solution.py:438
  66.9 1.5 %collective-permute-start.21 = (bf16[528,128]{1,0:T(8,128)(2,1)S(1)}, bf16[528,128]{1,0:T(8,128)(2,1)S(1)}, u32[]{:S(2)}, u32[]{:S(2)}) collective-permute-start(bf16[528,128]{1,0:T(8,128)(2,1)S(1)} %get-tuple-element.58), channel_id=1, source_target_pairs={{0,96},{32,0},{64,32},{96,64},{1,97},{33,1},{65,33},{97,65},{2,98}... | collective-permute-start | bytes 405512 | tf_op jit(solution)/shard_map/ppermute | solution.py:438
  68.4 1.8 %side.1 = (bf16[512,512]{1,0:T(8,128)(2,1)S(1)}, bf16[512,512]{1,0:T(8,128)(2,1)S(1)}, bf16[512,512]{1,0:T(8,128)(2,1)S(1)}, f32[128,512]{1,0:T(8,128)S(1)}, f32...) custom-call(s32[4,128]{1,0:T(4,128)S(1)} %collective-permute-done.meta.ints, ...), custom_call_target="tpu_custom_call" | custom-call | flops 1000000000 | bytes 4329984 | tf_op jit(solution)/shard_map/side/pallas_call | solution.py:58
  70.2 2.3 %slopes.2 = (bf16[4,512,384]{2,1,0:T(8,128)(2,1)S(1)}, bf16[4,512,512]{2,1,0:T(8,128)(2,1)S(1)}, bf16[4,128,512]{2,1,0:T(8,128)(2,1)S(1)}) custom-call(s32[4,128]{1,0:T(4,128)S(1)} %collective-permute-done.meta.ints, bf16[512,512]{1,0:T(8,128)(2,1)S(1)} %tie.4.n0, bf16[512,512]{1,0:T(8,128)(2,1)S(1)} %tie.6.na, bf16[512,512]{1,0:T(8,128)(2,1)S(1)} %tie.7.nb, ...), custom_call_target="tpu_custom_call" | custom-call | flops 1000000000 | bytes 6821888 | tf_op jit(solution)/shard_map/slopes/pallas_call | solution.py:58
  73.1 1.2 collective-permute-done.21.r3
  74.3 3.2 %middle.1 = (bf16[512,128]{1,0:T(8,128)(2,1)S(1)}, bf16[512,128]{1,0:T(8,128)(2,1)S(1)}, bf16[512,128]{1,0:T(8,128)(2,1)S(1)}, bf16[512,128]{1,0:T(8,128)(2,1)S(...) custom-call(s32[4,128]{1,0:T(4,128)S(1)} %collective-permute-done.me, ...), custom_call_target="tpu_custom_call" | custom-call | flops 1000000000 | bytes 5788672 | tf_op jit(solution)/shard_map/middle/pallas_call | solution.py:58
  77.6 3.5 %collective-permute-start.26 = (bf16[512,128]{1,0:T(8,128)(2,1)S(1)}, bf16[512,128]{1,0:T(8,128)(2,1)S(1)}, u32[]{:S(2)}, u32[]{:S(2)}) collective-permute-start(bf16[512,128]{1,0:T(8,128)(2,1)S(1)} %get-tuple-element.82), channel_id=1, source_target_pairs={{0,64},{32,96},{64,0},{96,32},{1,65},{33,97},{65,1},{97,33},{2,66}... | collective-permute-start | bytes 393224 | tf_op jit(solution)/shard_map/ppermute | solution.py:438
  81.3 2.9 %grads.1 = (bf16[512,640]{1,0:T(8,128)(2,1)S(1)}, bf16[512,640]{1,0:T(8,128)(2,1)S(1)}, bf16[512,128]{1,0:T(8,128)(2,1)S(1)}, bf16[512,128]{1,0:T(8,128)(2,1)S(1)}) custom-call(s32[4,128]{1,0:T(4,128)S(1)} %collective-permute-done.meta.ints, bf16[512,512]{1,0:T(8,128)(2,1)S(1)} %tie.4.n0, bf16[512,512]{1,0:T(8,128)(2,1)S(1)} %get-tuple-element.65.dpre, ...), custom_call_target="tpu_custom_call" | custom-call | flops 2000000000 | bytes 4329984 | tf_op jit(solution)/shard_map/grads/pallas_call | solution.py:58
  84.2 2.3 %collective-permute-start.24 = (bf16[512,640]{1,0:T(8,128)(2,1)S(1)}, bf16[512,640]{1,0:T(8,128)(2,1)S(1)}, u32[]{:S(2)}, u32[]{:S(2)}) collective-permute-start(bf16[512,640]{1,0:T(8,128)(2,1)S(1)} %get-tuple-element.76), channel_id=1, source_target_pairs={{0,1},{1,0},{2,3},{3,2},{4,5},{5,4},{6,7},{7,6},{8,9},{9,8},{10,11... | collective-permute-start | bytes 1966088 | tf_op jit(solution)/shard_map/ppermute | solution.py:434
  86.5 1.9 %slopes.3 = (bf16[4,512,256]{2,1,0:T(8,128)(2,1)S(1)}, bf16[4,512,512]{2,1,0:T(8,128)(2,1)S(1)}, bf16[4,128,512]{2,1,0:T(8,128)(2,1)S(1)}) custom-call(s32[4,128]{1,0:T(4,128)S(1)} %collective-permute-done.meta.ints, bf16[512,512]{1,0:T(8,128)(2,1)S(1)} %collective-permute-done.15.o0.n0, bf16[512,512]{1,0:T(8,128)(2,1)S(1)} %collective-permute-done.16.oa.na, ...), custom_call_target="tpu_custom_call" | custom-call | flops 1000000000 | bytes 6293504 | tf_op jit(solution)/shard_map/slopes/pallas_call | solution.py:58
  88.4 14.0 %backward.1 = (bf16[512,256]{1,0:T(8,128)(2,1)S(1)}, bf16[512,256]{1,0:T(8,128)(2,1)S(1)}) custom-call(s32[4,128]{1,0:T(4,128)S(1)} %collective-permute-done.meta.ints, bf16[4,512,128]{2,1,0:T(8,128)(2,1)S(1)} %get-tuple-element.77.q_s, bf16[8,512,128]{2,1,0:T(8,128)(2,1)S(1)} %get-tuple-element.78.k_s, bf16[8,512,128]{2,1,0:T(8,128)(2,1)S(1)} %get-tuple-element.79.v_s, ...), custom_call_target="tpu_custom_call" | custom-call | flops 10000000000 | bytes 11798528 | tf_op jit(solution)/shard_map/backward/pallas_call | solution.py:58
  102.4 4.3 %collective-permute-start.28 = (bf16[512,256]{1,0:T(8,128)(2,1)S(1)}, bf16[512,256]{1,0:T(8,128)(2,1)S(1)}, u32[]{:S(2)}, u32[]{:S(2)}) collective-permute-start(bf16[512,256]{1,0:T(8,128)(2,1)S(1)} %get-tuple-element.93), channel_id=1, source_target_pairs={{0,1},{1,0},{2,3},{3,2},{4,5},{5,4},{6,7},{7,6},{8,9},{9,8},{10,11... | collective-permute-start | bytes 786440 | tf_op jit(solution)/shard_map/ppermute | solution.py:434
  106.7 1.2 collective-permute-done.28
  108.2 30.5 %all_to_all.11 = bf16[64,8,896]{2,1,0:T(8,128)(2,1)S(1)} all-to-all(bf16[64,8,896]{2,1,0:T(8,128)(2,1)S(1)} %maximum_bitcast_fusion), channel_id=1, replica_groups=mesh['y'=4,'xh'=2,'xl'=2,'z'=4,'core'=2] {'y','xh','xl','z'}, dimensions={0} | all-to-all | bytes 1835008 | tf_op jit(solution)/shard_map/all_to_all | solution.py:582
  (84 shorter events, 8.7 us)
Async XLA Ops:
  2.1 1.8 %collective-permute-start.2 = (bf16[4,2560]{1,0:T(4,128)(2,1)S(1)}, bf16[4,2560]{1,0:T(4,128)(2,1)S(1)}, u32[]{:S(2)}, u32[]{:S(2)}) collective-permute-start(bf16[4,2560]{1,0:T(4,128)(2,1)S(1)} %constant_dynamic-update-slice_fusion), channel_id=1, source_target_pairs={{0,1},{1,0},{2,3},{3,2},{4,5},{5,4},{6,7},{7,6},{8,9},{9,8},{10,11... | collective-permute-start | bytes 61448 | tf_op jit(solution)/shard_map/ppermute | solution.py:434
  2.1 11.3 %collective-permute-start.1 = (bf16[512,512]{1,0:T(8,128)(2,1)}, bf16[512,512]{1,0:T(8,128)(2,1)S(1)}, u32[]{:S(2)}, u32[]{:S(2)}) collective-permute-start(bf16[512,512]{1,0:T(8,128)(2,1)} %bitcast.19), channel_id=1, source_target_pairs={{0,0},{1,16},{2,2},{3,18},{4,4},{5,20},{6,6},{7,22},{8,8},{9,24},{... | collective-permute-start | bytes 1572872 | tf_op jit(solution)/shard_map/ppermute | solution.py:430
  3.9 6.1 %collective-permute-start.3 = (bf16[8,2048]{1,0:T(8,128)(2,1)S(1)}, bf16[8,2048]{1,0:T(8,128)(2,1)S(1)}, u32[]{:S(2)}, u32[]{:S(2)}) collective-permute-start(bf16[8,2048]{1,0:T(8,128)(2,1)S(1)} %pad_maximum_fusion.1), channel_id=1, source_target_pairs={{0,96},{32,0},{64,32},{96,64},{1,97},{33,1},{65,33},{97,65},{2,98}... | collective-permute-start | bytes 98312 | tf_op jit(solution)/shard_map/ppermute | solution.py:442
  7.8 5.5 %collective-permute-start.5 = (bf16[8,2048]{1,0:T(8,128)(2,1)S(1)}, bf16[8,2048]{1,0:T(8,128)(2,1)S(1)}, u32[]{:S(2)}, u32[]{:S(2)}) collective-permute-start(bf16[8,2048]{1,0:T(8,128)(2,1)S(1)} %pad_maximum_fusion.1), channel_id=1, source_target_pairs={{0,32},{32,64},{64,96},{96,0},{1,33},{33,65},{65,97},{97,1},{2,34}... | collective-permute-start | bytes 98312 | tf_op jit(solution)/shard_map/ppermute | solution.py:442
  7.8 5.5 %collective-permute-start.4 = (bf16[8,2048]{1,0:T(8,128)(2,1)S(1)}, bf16[8,2048]{1,0:T(8,128)(2,1)S(1)}, u32[]{:S(2)}, u32[]{:S(2)}) collective-permute-start(bf16[8,2048]{1,0:T(8,128)(2,1)S(1)} %pad_maximum_fusion.1), channel_id=1, source_target_pairs={{0,64},{32,96},{64,0},{96,32},{1,65},{33,97},{65,1},{97,33},{2,66}... | collective-permute-start | bytes 98312 | tf_op jit(solution)/shard_map/ppermute | solution.py:442
  13.7 12.9 %collective-permute-start.12 = (bf16[512,512]{1,0:T(8,128)(2,1)S(1)}, bf16[512,512]{1,0:T(8,128)(2,1)S(1)}, u32[]{:S(2)}, u32[]{:S(2)}) collective-permute-start(bf16[512,512]{1,0:T(8,128)(2,1)S(1)} %norm.1.__0_), channel_id=1, source_target_pairs={{0,32},{1,97},{32,64},{33,1},{64,96},{65,33},{96,0},{97,65},{2,34}... | collective-permute-start | bytes 1572872 | tf_op jit(solution)/shard_map/ppermute | solution.py:459
  14.4 8.3 %collective-permute-start.8 = (bf16[32,896]{1,0:T(8,128)(2,1)S(1)}, bf16[32,896]{1,0:T(8,128)(2,1)S(1)}, u32[]{:S(2)}, u32[]{:S(2)}) collective-permute-start(bf16[32,896]{1,0:T(8,128)(2,1)S(1)} %pad_maximum_fusion.q0), channel_id=1, source_target_pairs={{0,24},{8,0},{16,8},{24,16},{1,25},{9,1},{17,9},{25,17},{2,26},{10... | collective-permute-start | bytes 172040 | tf_op jit(solution)/shard_map/ppermute | solution.py:442
  19.3 6.0 %collective-permute-start.7 = (bf16[32,896]{1,0:T(8,128)(2,1)S(1)}, bf16[32,896]{1,0:T(8,128)(2,1)S(1)}, u32[]{:S(2)}, u32[]{:S(2)}) collective-permute-start(bf16[32,896]{1,0:T(8,128)(2,1)S(1)} %pad_maximum_fusion.q0), channel_id=1, source_target_pairs={{0,16},{8,24},{16,0},{24,8},{1,17},{9,25},{17,1},{25,9},{2,18},{10... | collective-permute-start | bytes 172040 | tf_op jit(solution)/shard_map/ppermute | solution.py:442
  19.6 6.4 %collective-permute-start.6 = (bf16[32,896]{1,0:T(8,128)(2,1)S(1)}, bf16[32,896]{1,0:T(8,128)(2,1)S(1)}, u32[]{:S(2)}, u32[]{:S(2)}) collective-permute-start(bf16[32,896]{1,0:T(8,128)(2,1)S(1)} %pad_maximum_fusion.q0), channel_id=1, source_target_pairs={{0,8},{8,16},{16,24},{24,0},{1,9},{9,17},{17,25},{25,1},{2,10},{10... | collective-permute-start | bytes 172040 | tf_op jit(solution)/shard_map/ppermute | solution.py:442
  21.0 25.4 %collective-permute-start.14 = (bf16[512,512]{1,0:T(8,128)(2,1)S(1)}, bf16[512,512]{1,0:T(8,128)(2,1)S(1)}, u32[]{:S(2)}, u32[]{:S(2)}) collective-permute-start(bf16[512,512]{1,0:T(8,128)(2,1)S(1)} %norm.1.__0_), channel_id=1, source_target_pairs={{0,96},{1,33},{32,0},{33,65},{64,32},{65,97},{96,64},{97,1},{2,98}... | collective-permute-start | bytes 1572872 | tf_op jit(solution)/shard_map/ppermute | solution.py:459
  26.6 20.5 %collective-permute-start.13 = (bf16[512,512]{1,0:T(8,128)(2,1)S(1)}, bf16[512,512]{1,0:T(8,128)(2,1)S(1)}, u32[]{:S(2)}, u32[]{:S(2)}) collective-permute-start(bf16[512,512]{1,0:T(8,128)(2,1)S(1)} %tie.5.__0_), channel_id=1, source_target_pairs={{0,32},{1,97},{32,64},{33,1},{64,96},{65,33},{96,0},{97,65},{2,34}... | collective-permute-start | bytes 1572872 | tf_op jit(solution)/shard_map/ppermute | solution.py:459
  27.8 14.4 %collective-permute-start.11 = (bf16[128,896]{1,0:T(8,128)(2,1)S(1)}, bf16[128,896]{1,0:T(8,128)(2,1)S(1)}, u32[]{:S(2)}, u32[]{:S(2)}) collective-permute-start(bf16[128,896]{1,0:T(8,128)(2,1)S(1)} %plane.1.q0.__1_), channel_id=1, source_target_pairs={{0,6},{2,0},{4,2},{6,4},{1,7},{3,1},{5,3},{7,5},{8,14},{10,8},{12,... | collective-permute-start | bytes 688136 | tf_op jit(solution)/shard_map/ppermute | solution.py:442
  31.9 10.4 %collective-permute-start.10 = (bf16[128,896]{1,0:T(8,128)(2,1)S(1)}, bf16[128,896]{1,0:T(8,128)(2,1)S(1)}, u32[]{:S(2)}, u32[]{:S(2)}) collective-permute-start(bf16[128,896]{1,0:T(8,128)(2,1)S(1)} %plane.1.q0.__1_), channel_id=1, source_target_pairs={{0,4},{2,6},{4,0},{6,2},{1,5},{3,7},{5,1},{7,3},{8,12},{10,14},{12... | collective-permute-start | bytes 688136 | tf_op jit(solution)/shard_map/ppermute | solution.py:442
  31.9 13.8 %collective-permute-start.9 = (bf16[128,896]{1,0:T(8,128)(2,1)S(1)}, bf16[128,896]{1,0:T(8,128)(2,1)S(1)}, u32[]{:S(2)}, u32[]{:S(2)}) collective-permute-start(bf16[128,896]{1,0:T(8,128)(2,1)S(1)} %plane.1.q0.__1_), channel_id=1, source_target_pairs={{0,2},{2,4},{4,6},{6,0},{1,3},{3,5},{5,7},{7,1},{8,10},{10,12},{12... | collective-permute-start | bytes 688136 | tf_op jit(solution)/shard_map/ppermute | solution.py:442
  46.5 7.6 %collective-permute-start.17 = (bf16[512,512]{1,0:T(8,128)(2,1)S(1)}, bf16[512,512]{1,0:T(8,128)(2,1)S(1)}, u32[]{:S(2)}, u32[]{:S(2)}) collective-permute-start(bf16[512,512]{1,0:T(8,128)(2,1)S(1)} %tie.7.nb), channel_id=1, source_target_pairs={{0,1},{1,0},{2,3},{3,2},{4,5},{5,4},{6,7},{7,6},{8,9},{9,8},{10,11... | collective-permute-start | bytes 1572872 | tf_op jit(solution)/shard_map/ppermute | solution.py:434
  46.6 8.4 %collective-permute-start.15 = (bf16[512,512]{1,0:T(8,128)(2,1)S(1)}, bf16[512,512]{1,0:T(8,128)(2,1)S(1)}, u32[]{:S(2)}, u32[]{:S(2)}) collective-permute-start(bf16[512,512]{1,0:T(8,128)(2,1)S(1)} %tie.4.n0), channel_id=1, source_target_pairs={{0,1},{1,0},{2,3},{3,2},{4,5},{5,4},{6,7},{7,6},{8,9},{9,8},{10,11... | collective-permute-start | bytes 1572872 | tf_op jit(solution)/shard_map/ppermute | solution.py:434
  47.1 7.9 %collective-permute-start.16 = (bf16[512,512]{1,0:T(8,128)(2,1)S(1)}, bf16[512,512]{1,0:T(8,128)(2,1)S(1)}, u32[]{:S(2)}, u32[]{:S(2)}) collective-permute-start(bf16[512,512]{1,0:T(8,128)(2,1)S(1)} %tie.6.na), channel_id=1, source_target_pairs={{0,1},{1,0},{2,3},{3,2},{4,5},{5,4},{6,7},{7,6},{8,9},{9,8},{10,11... | collective-permute-start | bytes 1572872 | tf_op jit(solution)/shard_map/ppermute | solution.py:434
  47.2 7.8 %collective-permute-start.18 = (bf16[512,512]{1,0:T(8,128)(2,1)S(1)}, bf16[512,512]{1,0:T(8,128)(2,1)S(1)}, u32[]{:S(2)}, u32[]{:S(2)}) collective-permute-start(bf16[512,512]{1,0:T(8,128)(2,1)S(1)} %collective-permute-done.13.__1_.nc), channel_id=1, source_target_pairs={{0,1},{1,0},{2,3},{3,2},{4,5},{5,4},{6,7},{7,6},{8,9},{9,8},{10,11... | collective-permute-start | bytes 1572872 | tf_op jit(solution)/shard_map/ppermute | solution.py:434
  47.6 0.7 collective-permute-start
  48.3 20.1 %collective-permute-start.22 = (bf16[512,512]{1,0:T(8,128)(2,1)S(1)}, bf16[512,512]{1,0:T(8,128)(2,1)S(1)}, u32[]{:S(2)}, u32[]{:S(2)}) collective-permute-start(bf16[512,512]{1,0:T(8,128)(2,1)S(1)} %get-tuple-element.59.w_mine), channel_id=1, source_target_pairs={{0,1},{1,0},{2,3},{3,2},{4,5},{5,4},{6,7},{7,6},{8,9},{9,8},{10,11... | collective-permute-start | bytes 1572872 | tf_op jit(solution)/shard_map/ppermute | solution.py:434
  54.2 14.2 %copy-start.1 = (f32[256,128]{1,0:T(8,128)S(1)}, f32[256,128]{1,0:T(8,128)}, u32[]{:S(2)}) copy-start(f32[256,128]{1,0:T(8,128)} %table.1) | copy-start | bytes 393220
  54.2 14.2 %copy-start.2 = (f32[128,128]{1,0:T(8,128)S(1)}, f32[128,128]{1,0:T(8,128)}, u32[]{:S(2)}) copy-start(f32[128,128]{1,0:T(8,128)} %bias_w1.3) | copy-start | bytes 196612
  54.2 14.2 %copy-start.4 = (f32[128]{0:T(128)S(1)}, f32[128]{0:T(128)}, u32[]{:S(2)}) copy-start(f32[128]{0:T(128)} %param.25) | copy-start | bytes 1540
  54.2 18.3 %collective-permute-start.23 = (bf16[512,512]{1,0:T(8,128)(2,1)S(1)}, bf16[512,512]{1,0:T(8,128)(2,1)S(1)}, u32[]{:S(2)}, u32[]{:S(2)}) collective-permute-start(bf16[512,512]{1,0:T(8,128)(2,1)S(1)} %bitcast.20), channel_id=1, source_target_pairs={{0,0},{1,16},{2,2},{3,18},{4,4},{5,20},{6,6},{7,22},{8,8},{9,24},{... | collective-permute-start | bytes 1572872 | tf_op jit(solution)/shard_map/ppermute | solution.py:430
  65.1 8.0 %collective-permute-start.19 = (bf16[528,128]{1,0:T(8,128)(2,1)S(1)}, bf16[528,128]{1,0:T(8,128)(2,1)S(1)}, u32[]{:S(2)}, u32[]{:S(2)}) collective-permute-start(bf16[528,128]{1,0:T(8,128)(2,1)S(1)} %get-tuple-element.56), channel_id=1, source_target_pairs={{0,32},{32,64},{64,96},{96,0},{1,33},{33,65},{65,97},{97,1},{2,34}... | collective-permute-start | bytes 405512 | tf_op jit(solution)/shard_map/ppermute | solution.py:438
  65.5 7.6 %collective-permute-start.20 = (bf16[528,128]{1,0:T(8,128)(2,1)S(1)}, bf16[528,128]{1,0:T(8,128)(2,1)S(1)}, u32[]{:S(2)}, u32[]{:S(2)}) collective-permute-start(bf16[528,128]{1,0:T(8,128)(2,1)S(1)} %get-tuple-element.57), channel_id=1, source_target_pairs={{0,64},{32,96},{64,0},{96,32},{1,65},{33,97},{65,1},{97,33},{2,66}... | collective-permute-start | bytes 405512 | tf_op jit(solution)/shard_map/ppermute | solution.py:438
  66.9 7.4 %collective-permute-start.21 = (bf16[528,128]{1,0:T(8,128)(2,1)S(1)}, bf16[528,128]{1,0:T(8,128)(2,1)S(1)}, u32[]{:S(2)}, u32[]{:S(2)}) collective-permute-start(bf16[528,128]{1,0:T(8,128)(2,1)S(1)} %get-tuple-element.58), channel_id=1, source_target_pairs={{0,96},{32,0},{64,32},{96,64},{1,97},{33,1},{65,33},{97,65},{2,98}... | collective-permute-start | bytes 405512 | tf_op jit(solution)/shard_map/ppermute | solution.py:438
  77.5 10.9 %collective-permute-start.25 = (bf16[512,128]{1,0:T(8,128)(2,1)S(1)}, bf16[512,128]{1,0:T(8,128)(2,1)S(1)}, u32[]{:S(2)}, u32[]{:S(2)}) collective-permute-start(bf16[512,128]{1,0:T(8,128)(2,1)S(1)} %get-tuple-element.81), channel_id=1, source_target_pairs={{0,32},{32,64},{64,96},{96,0},{1,33},{33,65},{65,97},{97,1},{2,34}... | collective-permute-start | bytes 393224 | tf_op jit(solution)/shard_map/ppermute | solution.py:438
  77.6 10.8 %collective-permute-start.26 = (bf16[512,128]{1,0:T(8,128)(2,1)S(1)}, bf16[512,128]{1,0:T(8,128)(2,1)S(1)}, u32[]{:S(2)}, u32[]{:S(2)}) collective-permute-start(bf16[512,128]{1,0:T(8,128)(2,1)S(1)} %get-tuple-element.82), channel_id=1, source_target_pairs={{0,64},{32,96},{64,0},{96,32},{1,65},{33,97},{65,1},{97,33},{2,66}... | collective-permute-start | bytes 393224 | tf_op jit(solution)/shard_map/ppermute | solution.py:438
  81.0 7.4 %collective-permute-start.27 = (bf16[512,128]{1,0:T(8,128)(2,1)S(1)}, bf16[512,128]{1,0:T(8,128)(2,1)S(1)}, u32[]{:S(2)}, u32[]{:S(2)}) collective-permute-start(bf16[512,128]{1,0:T(8,128)(2,1)S(1)} %get-tuple-element.83), channel_id=1, source_target_pairs={{0,96},{32,0},{64,32},{96,64},{1,97},{33,1},{65,33},{97,65},{2,98}... | collective-permute-start | bytes 393224 | tf_op jit(solution)/shard_map/ppermute | solution.py:438
  84.2 23.7 %collective-permute-start.24 = (bf16[512,640]{1,0:T(8,128)(2,1)S(1)}, bf16[512,640]{1,0:T(8,128)(2,1)S(1)}, u32[]{:S(2)}, u32[]{:S(2)}) collective-permute-start(bf16[512,640]{1,0:T(8,128)(2,1)S(1)} %get-tuple-element.76), channel_id=1, source_target_pairs={{0,1},{1,0},{2,3},{3,2},{4,5},{5,4},{6,7},{7,6},{8,9},{9,8},{10,11... | collective-permute-start | bytes 1966088 | tf_op jit(solution)/shard_map/ppermute | solution.py:434
  102.4 5.4 %collective-permute-start.28 = (bf16[512,256]{1,0:T(8,128)(2,1)S(1)}, bf16[512,256]{1,0:T(8,128)(2,1)S(1)}, u32[]{:S(2)}, u32[]{:S(2)}) collective-permute-start(bf16[512,256]{1,0:T(8,128)(2,1)S(1)} %get-tuple-element.93), channel_id=1, source_target_pairs={{0,1},{1,0},{2,3},{3,2},{4,5},{5,4},{6,7},{7,6},{8,9},{9,8},{10,11... | collective-permute-start | bytes 786440 | tf_op jit(solution)/shard_map/ppermute | solution.py:434
  (6 other events, 19.4 us)
where the time goes:
time: 140 us; the launch traced here: 139 us
  starting transfers between devices  44.5 us (32%)
  Pallas kernels  38.4 us (27%)
  blocking collectives  30.5 us (22%)
  waiting for transfers between devices  22.1 us (16%)
  local copies, waits for them, and re-layouts  1.62 us (1%)
    pallas_call x11, Pallas kernels, call(): pl.pallas_call(kernel, out_shape=tuple(outs), in_specs=smem() * n_smem +...  38.4 us
    all_to_all x1, blocking collectives, body(): got = lax.all_to_all(pair, CHIPS, 0, 0, tiled=True)  30.5 us
    ppermute x9, waiting for transfers between devices, moved(): return lax.ppermute(x, axes, [(i, (i + k) % 4) for i in range(4)])  19.1 us
    ppermute x9, starting transfers between devices, moved(): return lax.ppermute(x, axes, [(i, (i + k) % 4) for i in range(4)])  17.2 us
    ppermute x8, starting transfers between devices, across(): return lax.ppermute(x, 'core', [(0, 1), (1, 0)])  13.5 us
    ppermute x6, starting transfers between devices, ring(): return lax.ppermute(x, 'y', [(i, (i + k) % 4) for i in range(4)])  7.16 us
    ppermute x3, starting transfers between devices, turned(): lax.ppermute(x, ('y', 'core'), [(2 * i + c, 2 * ((i + (k if c == 0 else -...  3.47 us
    ppermute x3, starting transfers between devices, swapped(): return lax.ppermute(x, ('xh', 'xl', 'z', 'core'), SWAP)  3.18 us
  transfers between devices with their start and end apart: 29, of which 8 were waited for; matrix products, arithmetic and copies ran while one was open for 1% of the time, Pallas kernels for 24%

commit v1 on v0

--- a/solution.py
+++ b/solution.py
@@ -480,7 +480,10 @@
     line = jnp.concatenate(
         [lax.dynamic_slice_in_dim(line, at + y * E, E, 1) for at in (W, 2 * W, 0)] + [line[:, 3 * W :]], axis=1
     )
-    coords = jnp.stack([y, x, z]).astype(I32)
+    lens = jnp.where(core == lax.axis_index("xh"), lengths, across(lengths))
+    coords = jnp.concatenate([jnp.stack([y, x, z]).astype(I32), lens[0], core.astype(I32)[None]])
+    early_meta = jnp.concatenate([coords[0:1], coords[7:8], coords[3:7]])[None]
+    early_meta = jnp.broadcast_to(early_meta, (4, 6))
     (plane,) = call(
         plane_kernel,
         [sds((E, 7 * E), BF16)],
@@ -516,7 +519,7 @@
 
     qkv = [sds((4, R, E), BF16), sds((8, R, E), BF16), sds((8, R, E), BF16)]
     a0, a1, a2, a3, q_s, k_s, v_s = call(
-        forward_kernel, [sds((R + 16, E), BF16)] * 4 + qkv, [meta] + parts + [wg], flops=5 * 10**9,
+        forward_kernel, [sds((R + 16, E), BF16)] * 4 + qkv, [early_meta] + parts + [wg], flops=5 * 10**9,
         scratch=[pltpu.VMEM((4, R + 16, E), BF16)], name="forward",
     )
     r1, r2, r3 = ring(a1, 1), ring(a2, 2), ring(a3, 3)

time: 140 us -> 137 us (0.979)
  blocking collectives: 30.5 us -> 28.1 us
    all_to_all x1, blocking collectives: 30.5 us -> 28.1 us  [body(): got = lax.all_to_all(pair, CHIPS, 0, 0, tiled=True)]
    ppermute x8 -> x9, starting transfers between devices: 13.5 us -> 11.8 us  [across(): return lax.ppermute(x, 'core', [(0, 1), (1, 0)])]
    ppermute x8 -> x9, waiting for transfers between devices: 1.18 us -> 2.67 us  [across(): return lax.ppermute(x, 'core', [(0, 1), (1, 0)])]
  transfers between devices with their start and end apart: 29 -> 30, of which waited for: 8 -> 12; matrix products, arithmetic and copies ran while one was open for 1% -> 2% of each run, Pallas kernels for 24% -> 25%
where the time goes in v1:
time: 137 us
  starting transfers between devices  43.1 us (31%)
  Pallas kernels  38.4 us (28%)
  blocking collectives  28.1 us (21%)
  waiting for transfers between devices  23.3 us (17%)
  local copies, waits for them, and re-layouts  1.71 us (1%)
    pallas_call x11, Pallas kernels, call(): pl.pallas_call(kernel, out_shape=tuple(outs), in_specs=smem() * n_smem +...  38.4 us
    all_to_all x1, blocking collectives, body(): got = lax.all_to_all(pair, CHIPS, 0, 0, tiled=True)  28.1 us
    ppermute x9, waiting for transfers between devices, moved(): return lax.ppermute(x, axes, [(i, (i + k) % 4) for i in range(4)])  19.3 us
    ppermute x9, starting transfers between devices, moved(): return lax.ppermute(x, axes, [(i, (i + k) % 4) for i in range(4)])  17.2 us
    ppermute x9, starting transfers between devices, across(): return lax.ppermute(x, 'core', [(0, 1), (1, 0)])  11.8 us
    ppermute x6, starting transfers between devices, ring(): return lax.ppermute(x, 'y', [(i, (i + k) % 4) for i in range(4)])  7.76 us
    ppermute x3, starting transfers between devices, turned(): lax.ppermute(x, ('y', 'core'), [(2 * i + c, 2 * ((i + (k if c == 0 else -...  3.27 us
    ppermute x3, starting transfers between devices, swapped(): return lax.ppermute(x, ('xh', 'xl', 'z', 'core'), SWAP)  3.02 us
  transfers between devices with their start and end apart: 30, of which 12 were waited for; matrix products, arithmetic and copies ran while one was open for 2% of the time, Pallas kernels for 25%

profile of v1, /device:TPU:0, one launch (start us, length us, event | category | flops | bytes accessed | tf_op | source)
XLA Modules:
  0.0 136.8 jit_solution(8084365078607733311)
XLA Ops:
  2.7 1.7 %collective-permute-start.1 = (bf16[512,512]{1,0:T(8,128)(2,1)}, bf16[512,512]{1,0:T(8,128)(2,1)S(1)}, u32[]{:S(2)}, u32[]{:S(2)}) collective-permute-start(bf16[512,512]{1,0:T(8,128)(2,1)} %bitcast.22), channel_id=1, source_target_pairs={{0,0},{1,16},{2,2},{3,18},{4,4},{5,20},{6,6},{7,22},{8,8},{9,24},{... | collective-permute-start | bytes 1572872 | tf_op jit(solution)/shard_map/ppermute | solution.py:430
  4.5 3.2 %collective-permute-start.4 = (bf16[8,2048]{1,0:T(8,128)(2,1)S(1)}, bf16[8,2048]{1,0:T(8,128)(2,1)S(1)}, u32[]{:S(2)}, u32[]{:S(2)}) collective-permute-start(bf16[8,2048]{1,0:T(8,128)(2,1)S(1)} %pad_maximum_fusion.1), channel_id=1, source_target_pairs={{0,96},{32,0},{64,32},{96,64},{1,97},{33,1},{65,33},{97,65},{2,98}... | collective-permute-start | bytes 98312 | tf_op jit(solution)/shard_map/ppermute | solution.py:442
  8.4 2.2 %collective-permute-start.5 = (bf16[8,2048]{1,0:T(8,128)(2,1)S(1)}, bf16[8,2048]{1,0:T(8,128)(2,1)S(1)}, u32[]{:S(2)}, u32[]{:S(2)}) collective-permute-start(bf16[8,2048]{1,0:T(8,128)(2,1)S(1)} %pad_maximum_fusion.1), channel_id=1, source_target_pairs={{0,64},{32,96},{64,0},{96,32},{1,65},{33,97},{65,1},{97,33},{2,66}... | collective-permute-start | bytes 98312 | tf_op jit(solution)/shard_map/ppermute | solution.py:442
  10.6 3.3 %collective-permute-done.5 = bf16[8,2048]{1,0:T(8,128)(2,1)S(1)} collective-permute-done((bf16[8,2048]{1,0:T(8,128)(2,1)S(1)}, bf16[8,2048]{1,0:T(8,128)(2,1)S(1)}, u32[]{:S(2)}, u32[]{:S(2)}) %collective-permute-start.5) | collective-permute-done | bytes 32800 | tf_op jit(solution)/shard_map/ppermute | solution.py:442
  15.0 4.9 %collective-permute-start.9 = (bf16[32,896]{1,0:T(8,128)(2,1)S(1)}, bf16[32,896]{1,0:T(8,128)(2,1)S(1)}, u32[]{:S(2)}, u32[]{:S(2)}) collective-permute-start(bf16[32,896]{1,0:T(8,128)(2,1)S(1)} %pad_maximum_fusion.q0), channel_id=1, source_target_pairs={{0,24},{8,0},{16,8},{24,16},{1,25},{9,1},{17,9},{25,17},{2,26},{10... | collective-permute-start | bytes 172040 | tf_op jit(solution)/shard_map/ppermute | solution.py:442
  20.2 1.3 collective-permute-start.7
  21.7 1.7 %collective-permute-start.15 = (bf16[512,512]{1,0:T(8,128)(2,1)S(1)}, bf16[512,512]{1,0:T(8,128)(2,1)S(1)}, u32[]{:S(2)}, u32[]{:S(2)}) collective-permute-start(bf16[512,512]{1,0:T(8,128)(2,1)S(1)} %norm.1.__0_), channel_id=1, source_target_pairs={{0,96},{1,33},{32,0},{33,65},{64,32},{65,97},{96,64},{97,1},{2,98}... | collective-permute-start | bytes 1572872 | tf_op jit(solution)/shard_map/ppermute | solution.py:459
  23.3 2.5 %collective-permute-done.8.q2 = bf16[32,896]{1,0:T(8,128)(2,1)S(1)} collective-permute-done((bf16[32,896]{1,0:T(8,128)(2,1)S(1)}, bf16[32,896]{1,0:T(8,128)(2,1)S(1)}, u32[]{:S(2)}, u32[]{:S(2)}) %collective-permute-start.8) | collective-permute-done | bytes 57376 | tf_op jit(solution)/shard_map/ppermute | solution.py:442
  25.8 0.9 collective-permute-done.7.q1
  27.4 1.0 collective-permute-start.14
  28.4 4.0 %collective-permute-start.12 = (bf16[128,896]{1,0:T(8,128)(2,1)S(1)}, bf16[128,896]{1,0:T(8,128)(2,1)S(1)}, u32[]{:S(2)}, u32[]{:S(2)}) collective-permute-start(bf16[128,896]{1,0:T(8,128)(2,1)S(1)} %plane.1.q0.__1_), channel_id=1, source_target_pairs={{0,6},{2,0},{4,2},{6,4},{1,7},{3,1},{5,3},{7,5},{8,14},{10,8},{12,... | collective-permute-start | bytes 688136 | tf_op jit(solution)/shard_map/ppermute | solution.py:442
  32.5 1.3 collective-permute-start.10
  33.7 9.2 %collective-permute-done.12.q3 = bf16[128,896]{1,0:T(8,128)(2,1)S(1)} collective-permute-done((bf16[128,896]{1,0:T(8,128)(2,1)S(1)}, bf16[128,896]{1,0:T(8,128)(2,1)S(1)}, u32[]{:S(2)}, u32[]{:S(2)}) %collective-permute-start.12) | collective-permute-done | bytes 229408 | tf_op jit(solution)/shard_map/ppermute | solution.py:442
  42.9 3.4 %collective-permute-done.10.q1 = bf16[128,896]{1,0:T(8,128)(2,1)S(1)} collective-permute-done((bf16[128,896]{1,0:T(8,128)(2,1)S(1)}, bf16[128,896]{1,0:T(8,128)(2,1)S(1)}, u32[]{:S(2)}, u32[]{:S(2)}) %collective-permute-start.10) | collective-permute-done | bytes 229408 | tf_op jit(solution)/shard_map/ppermute | solution.py:442
  46.3 0.8 cube.1
  50.7 0.7 collective-permute-done.19.oc.nc
  51.4 10.0 %forward.1 = (bf16[528,128]{1,0:T(8,128)(2,1)S(1)}, bf16[528,128]{1,0:T(8,128)(2,1)S(1)}, bf16[528,128]{1,0:T(8,128)(2,1)S(1)}, bf16[528,128]{1,0:T(8,128)(2,1)S...) custom-call(s32[4,6]{1,0:T(4,128)S(1)} %broadcast_in_dim.14.meta, ...), custom_call_target="tpu_custom_call" | custom-call | flops 5000000000 | bytes 7749728 | tf_op jit(solution)/shard_map/forward/pallas_call | solution.py:58
  61.9 1.3 collective-permute-start.21
  63.3 1.5 %collective-permute-start.22 = (bf16[528,128]{1,0:T(8,128)(2,1)S(1)}, bf16[528,128]{1,0:T(8,128)(2,1)S(1)}, u32[]{:S(2)}, u32[]{:S(2)}) collective-permute-start(bf16[528,128]{1,0:T(8,128)(2,1)S(1)} %get-tuple-element.58), channel_id=1, source_target_pairs={{0,96},{32,0},{64,32},{96,64},{1,97},{33,1},{65,33},{97,65},{2,98}... | collective-permute-start | bytes 405512 | tf_op jit(solution)/shard_map/ppermute | solution.py:438
  64.8 1.8 %side.1 = (bf16[512,512]{1,0:T(8,128)(2,1)S(1)}, bf16[512,512]{1,0:T(8,128)(2,1)S(1)}, bf16[512,512]{1,0:T(8,128)(2,1)S(1)}, f32[128,512]{1,0:T(8,128)S(1)}, f32...) custom-call(s32[4,128]{1,0:T(4,128)S(1)} %collective-permute-done.meta.ints, ...), custom_call_target="tpu_custom_call" | custom-call | flops 1000000000 | bytes 4329984 | tf_op jit(solution)/shard_map/side/pallas_call | solution.py:58
  66.6 2.3 %slopes.2 = (bf16[4,512,384]{2,1,0:T(8,128)(2,1)S(1)}, bf16[4,512,512]{2,1,0:T(8,128)(2,1)S(1)}, bf16[4,128,512]{2,1,0:T(8,128)(2,1)S(1)}) custom-call(s32[4,128]{1,0:T(4,128)S(1)} %collective-permute-done.meta.ints, bf16[512,512]{1,0:T(8,128)(2,1)S(1)} %tie.4.n0, bf16[512,512]{1,0:T(8,128)(2,1)S(1)} %tie.6.na, bf16[512,512]{1,0:T(8,128)(2,1)S(1)} %tie.7.nb, ...), custom_call_target="tpu_custom_call" | custom-call | flops 1000000000 | bytes 6821888 | tf_op jit(solution)/shard_map/slopes/pallas_call | solution.py:58
  69.2 0.9 collective-permute-done.22.r3
  70.1 3.2 %middle.1 = (bf16[512,128]{1,0:T(8,128)(2,1)S(1)}, bf16[512,128]{1,0:T(8,128)(2,1)S(1)}, bf16[512,128]{1,0:T(8,128)(2,1)S(1)}, bf16[512,128]{1,0:T(8,128)(2,1)S(...) custom-call(s32[4,128]{1,0:T(4,128)S(1)} %collective-permute-done.me, ...), custom_call_target="tpu_custom_call" | custom-call | flops 1000000000 | bytes 5788672 | tf_op jit(solution)/shard_map/middle/pallas_call | solution.py:58
  73.9 3.3 %collective-permute-start.27 = (bf16[512,128]{1,0:T(8,128)(2,1)S(1)}, bf16[512,128]{1,0:T(8,128)(2,1)S(1)}, u32[]{:S(2)}, u32[]{:S(2)}) collective-permute-start(bf16[512,128]{1,0:T(8,128)(2,1)S(1)} %get-tuple-element.82), channel_id=1, source_target_pairs={{0,64},{32,96},{64,0},{96,32},{1,65},{33,97},{65,1},{97,33},{2,66}... | collective-permute-start | bytes 393224 | tf_op jit(solution)/shard_map/ppermute | solution.py:438
  77.7 2.9 %grads.1 = (bf16[512,640]{1,0:T(8,128)(2,1)S(1)}, bf16[512,640]{1,0:T(8,128)(2,1)S(1)}, bf16[512,128]{1,0:T(8,128)(2,1)S(1)}, bf16[512,128]{1,0:T(8,128)(2,1)S(1)}) custom-call(s32[4,128]{1,0:T(4,128)S(1)} %collective-permute-done.meta.ints, bf16[512,512]{1,0:T(8,128)(2,1)S(1)} %tie.4.n0, bf16[512,512]{1,0:T(8,128)(2,1)S(1)} %get-tuple-element.65.dpre, ...), custom_call_target="tpu_custom_call" | custom-call | flops 2000000000 | bytes 4329984 | tf_op jit(solution)/shard_map/grads/pallas_call | solution.py:58
  80.6 5.9 %collective-permute-start.25 = (bf16[512,640]{1,0:T(8,128)(2,1)S(1)}, bf16[512,640]{1,0:T(8,128)(2,1)S(1)}, u32[]{:S(2)}, u32[]{:S(2)}) collective-permute-start(bf16[512,640]{1,0:T(8,128)(2,1)S(1)} %get-tuple-element.76), channel_id=1, source_target_pairs={{0,1},{1,0},{2,3},{3,2},{4,5},{5,4},{6,7},{7,6},{8,9},{9,8},{10,11... | collective-permute-start | bytes 1966088 | tf_op jit(solution)/shard_map/ppermute | solution.py:434
  86.5 1.9 %slopes.3 = (bf16[4,512,256]{2,1,0:T(8,128)(2,1)S(1)}, bf16[4,512,512]{2,1,0:T(8,128)(2,1)S(1)}, bf16[4,128,512]{2,1,0:T(8,128)(2,1)S(1)}) custom-call(s32[4,128]{1,0:T(4,128)S(1)} %collective-permute-done.meta.ints, bf16[512,512]{1,0:T(8,128)(2,1)S(1)} %collective-permute-done.16.o0.n0, bf16[512,512]{1,0:T(8,128)(2,1)S(1)} %collective-permute-done.17.oa.na, ...), custom_call_target="tpu_custom_call" | custom-call | flops 1000000000 | bytes 6293504 | tf_op jit(solution)/shard_map/slopes/pallas_call | solution.py:58
  88.4 14.0 %backward.1 = (bf16[512,256]{1,0:T(8,128)(2,1)S(1)}, bf16[512,256]{1,0:T(8,128)(2,1)S(1)}) custom-call(s32[4,128]{1,0:T(4,128)S(1)} %collective-permute-done.meta.ints, bf16[4,512,128]{2,1,0:T(8,128)(2,1)S(1)} %get-tuple-element.77.q_s, bf16[8,512,128]{2,1,0:T(8,128)(2,1)S(1)} %get-tuple-element.78.k_s, bf16[8,512,128]{2,1,0:T(8,128)(2,1)S(1)} %get-tuple-element.79.v_s, ...), custom_call_target="tpu_custom_call" | custom-call | flops 10000000000 | bytes 11798528 | tf_op jit(solution)/shard_map/backward/pallas_call | solution.py:58
  102.4 4.0 %collective-permute-start.29 = (bf16[512,256]{1,0:T(8,128)(2,1)S(1)}, bf16[512,256]{1,0:T(8,128)(2,1)S(1)}, u32[]{:S(2)}, u32[]{:S(2)}) collective-permute-start(bf16[512,256]{1,0:T(8,128)(2,1)S(1)} %get-tuple-element.93), channel_id=1, source_target_pairs={{0,1},{1,0},{2,3},{3,2},{4,5},{5,4},{6,7},{7,6},{8,9},{9,8},{10,11... | collective-permute-start | bytes 786440 | tf_op jit(solution)/shard_map/ppermute | solution.py:434
  106.5 1.2 collective-permute-done.29
  108.0 28.1 %all_to_all.11 = bf16[64,8,896]{2,1,0:T(8,128)(2,1)S(1)} all-to-all(bf16[64,8,896]{2,1,0:T(8,128)(2,1)S(1)} %maximum_bitcast_fusion), channel_id=1, replica_groups=mesh['y'=4,'xh'=2,'xl'=2,'z'=4,'core'=2] {'y','xh','xl','z'}, dimensions={0} | all-to-all | bytes 1835008 | tf_op jit(solution)/shard_map/all_to_all | solution.py:585
  136.1 0.7 total.1
  (91 shorter events, 10.8 us)
Async XLA Ops:
  0.6 20.9 %copy-start.5 = (s32[1,4]{1,0:T(1,128)S(1)}, s32[1,4]{1,0:T(1,128)}, u32[]{:S(2)}) copy-start(s32[1,4]{1,0:T(1,128)} %param.14) | copy-start | bytes 52
  0.6 20.9 %collective-permute-start.2 = (s32[1,4]{1,0:T(1,128)}, s32[1,4]{1,0:T(1,128)S(1)}, u32[]{:S(2)}, u32[]{:S(2)}) collective-permute-start(s32[1,4]{1,0:T(1,128)} %param.14), channel_id=1, source_target_pairs={{0,1},{1,0},{2,3},{3,2},{4,5},{5,4},{6,7},{7,6},{8,9},{9,8},{10,11... | collective-permute-start | bytes 56 | tf_op jit(solution)/shard_map/ppermute | solution.py:434
  2.2 2.3 %collective-permute-start.3 = (bf16[4,2560]{1,0:T(4,128)(2,1)S(1)}, bf16[4,2560]{1,0:T(4,128)(2,1)S(1)}, u32[]{:S(2)}, u32[]{:S(2)}) collective-permute-start(bf16[4,2560]{1,0:T(4,128)(2,1)S(1)} %constant_dynamic-update-slice_fusion), channel_id=1, source_target_pairs={{0,1},{1,0},{2,3},{3,2},{4,5},{5,4},{6,7},{7,6},{8,9},{9,8},{10,11... | collective-permute-start | bytes 61448 | tf_op jit(solution)/shard_map/ppermute | solution.py:434
  2.7 11.3 %collective-permute-start.1 = (bf16[512,512]{1,0:T(8,128)(2,1)}, bf16[512,512]{1,0:T(8,128)(2,1)S(1)}, u32[]{:S(2)}, u32[]{:S(2)}) collective-permute-start(bf16[512,512]{1,0:T(8,128)(2,1)} %bitcast.22), channel_id=1, source_target_pairs={{0,0},{1,16},{2,2},{3,18},{4,4},{5,20},{6,6},{7,22},{8,8},{9,24},{... | collective-permute-start | bytes 1572872 | tf_op jit(solution)/shard_map/ppermute | solution.py:430
  4.5 6.1 %collective-permute-start.4 = (bf16[8,2048]{1,0:T(8,128)(2,1)S(1)}, bf16[8,2048]{1,0:T(8,128)(2,1)S(1)}, u32[]{:S(2)}, u32[]{:S(2)}) collective-permute-start(bf16[8,2048]{1,0:T(8,128)(2,1)S(1)} %pad_maximum_fusion.1), channel_id=1, source_target_pairs={{0,96},{32,0},{64,32},{96,64},{1,97},{33,1},{65,33},{97,65},{2,98}... | collective-permute-start | bytes 98312 | tf_op jit(solution)/shard_map/ppermute | solution.py:442
  8.4 5.5 %collective-permute-start.6 = (bf16[8,2048]{1,0:T(8,128)(2,1)S(1)}, bf16[8,2048]{1,0:T(8,128)(2,1)S(1)}, u32[]{:S(2)}, u32[]{:S(2)}) collective-permute-start(bf16[8,2048]{1,0:T(8,128)(2,1)S(1)} %pad_maximum_fusion.1), channel_id=1, source_target_pairs={{0,32},{32,64},{64,96},{96,0},{1,33},{33,65},{65,97},{97,1},{2,34}... | collective-permute-start | bytes 98312 | tf_op jit(solution)/shard_map/ppermute | solution.py:442
  8.4 5.5 %collective-permute-start.5 = (bf16[8,2048]{1,0:T(8,128)(2,1)S(1)}, bf16[8,2048]{1,0:T(8,128)(2,1)S(1)}, u32[]{:S(2)}, u32[]{:S(2)}) collective-permute-start(bf16[8,2048]{1,0:T(8,128)(2,1)S(1)} %pad_maximum_fusion.1), channel_id=1, source_target_pairs={{0,64},{32,96},{64,0},{96,32},{1,65},{33,97},{65,1},{97,33},{2,66}... | collective-permute-start | bytes 98312 | tf_op jit(solution)/shard_map/ppermute | solution.py:442
  14.3 13.0 %collective-permute-start.13 = (bf16[512,512]{1,0:T(8,128)(2,1)S(1)}, bf16[512,512]{1,0:T(8,128)(2,1)S(1)}, u32[]{:S(2)}, u32[]{:S(2)}) collective-permute-start(bf16[512,512]{1,0:T(8,128)(2,1)S(1)} %norm.1.__0_), channel_id=1, source_target_pairs={{0,32},{1,97},{32,64},{33,1},{64,96},{65,33},{96,0},{97,65},{2,34}... | collective-permute-start | bytes 1572872 | tf_op jit(solution)/shard_map/ppermute | solution.py:459
  15.0 8.3 %collective-permute-start.9 = (bf16[32,896]{1,0:T(8,128)(2,1)S(1)}, bf16[32,896]{1,0:T(8,128)(2,1)S(1)}, u32[]{:S(2)}, u32[]{:S(2)}) collective-permute-start(bf16[32,896]{1,0:T(8,128)(2,1)S(1)} %pad_maximum_fusion.q0), channel_id=1, source_target_pairs={{0,24},{8,0},{16,8},{24,16},{1,25},{9,1},{17,9},{25,17},{2,26},{10... | collective-permute-start | bytes 172040 | tf_op jit(solution)/shard_map/ppermute | solution.py:442
  19.9 6.0 %collective-permute-start.8 = (bf16[32,896]{1,0:T(8,128)(2,1)S(1)}, bf16[32,896]{1,0:T(8,128)(2,1)S(1)}, u32[]{:S(2)}, u32[]{:S(2)}) collective-permute-start(bf16[32,896]{1,0:T(8,128)(2,1)S(1)} %pad_maximum_fusion.q0), channel_id=1, source_target_pairs={{0,16},{8,24},{16,0},{24,8},{1,17},{9,25},{17,1},{25,9},{2,18},{10... | collective-permute-start | bytes 172040 | tf_op jit(solution)/shard_map/ppermute | solution.py:442
  20.2 6.5 %collective-permute-start.7 = (bf16[32,896]{1,0:T(8,128)(2,1)S(1)}, bf16[32,896]{1,0:T(8,128)(2,1)S(1)}, u32[]{:S(2)}, u32[]{:S(2)}) collective-permute-start(bf16[32,896]{1,0:T(8,128)(2,1)S(1)} %pad_maximum_fusion.q0), channel_id=1, source_target_pairs={{0,8},{8,16},{16,24},{24,0},{1,9},{9,17},{17,25},{25,1},{2,10},{10... | collective-permute-start | bytes 172040 | tf_op jit(solution)/shard_map/ppermute | solution.py:442
  21.7 25.4 %collective-permute-start.15 = (bf16[512,512]{1,0:T(8,128)(2,1)S(1)}, bf16[512,512]{1,0:T(8,128)(2,1)S(1)}, u32[]{:S(2)}, u32[]{:S(2)}) collective-permute-start(bf16[512,512]{1,0:T(8,128)(2,1)S(1)} %norm.1.__0_), channel_id=1, source_target_pairs={{0,96},{1,33},{32,0},{33,65},{64,32},{65,97},{96,64},{97,1},{2,98}... | collective-permute-start | bytes 1572872 | tf_op jit(solution)/shard_map/ppermute | solution.py:459
  27.4 20.4 %collective-permute-start.14 = (bf16[512,512]{1,0:T(8,128)(2,1)S(1)}, bf16[512,512]{1,0:T(8,128)(2,1)S(1)}, u32[]{:S(2)}, u32[]{:S(2)}) collective-permute-start(bf16[512,512]{1,0:T(8,128)(2,1)S(1)} %tie.5.__0_), channel_id=1, source_target_pairs={{0,32},{1,97},{32,64},{33,1},{64,96},{65,33},{96,0},{97,65},{2,34}... | collective-permute-start | bytes 1572872 | tf_op jit(solution)/shard_map/ppermute | solution.py:459
  28.4 14.5 %collective-permute-start.12 = (bf16[128,896]{1,0:T(8,128)(2,1)S(1)}, bf16[128,896]{1,0:T(8,128)(2,1)S(1)}, u32[]{:S(2)}, u32[]{:S(2)}) collective-permute-start(bf16[128,896]{1,0:T(8,128)(2,1)S(1)} %plane.1.q0.__1_), channel_id=1, source_target_pairs={{0,6},{2,0},{4,2},{6,4},{1,7},{3,1},{5,3},{7,5},{8,14},{10,8},{12,... | collective-permute-start | bytes 688136 | tf_op jit(solution)/shard_map/ppermute | solution.py:442
  32.5 10.4 %collective-permute-start.11 = (bf16[128,896]{1,0:T(8,128)(2,1)S(1)}, bf16[128,896]{1,0:T(8,128)(2,1)S(1)}, u32[]{:S(2)}, u32[]{:S(2)}) collective-permute-start(bf16[128,896]{1,0:T(8,128)(2,1)S(1)} %plane.1.q0.__1_), channel_id=1, source_target_pairs={{0,4},{2,6},{4,0},{6,2},{1,5},{3,7},{5,1},{7,3},{8,12},{10,14},{12... | collective-permute-start | bytes 688136 | tf_op jit(solution)/shard_map/ppermute | solution.py:442
  32.5 13.8 %collective-permute-start.10 = (bf16[128,896]{1,0:T(8,128)(2,1)S(1)}, bf16[128,896]{1,0:T(8,128)(2,1)S(1)}, u32[]{:S(2)}, u32[]{:S(2)}) collective-permute-start(bf16[128,896]{1,0:T(8,128)(2,1)S(1)} %plane.1.q0.__1_), channel_id=1, source_target_pairs={{0,2},{2,4},{4,6},{6,0},{1,3},{3,5},{5,7},{7,1},{8,10},{10,12},{12... | collective-permute-start | bytes 688136 | tf_op jit(solution)/shard_map/ppermute | solution.py:442
  47.2 2.0 %collective-permute-start.18 = (bf16[512,512]{1,0:T(8,128)(2,1)S(1)}, bf16[512,512]{1,0:T(8,128)(2,1)S(1)}, u32[]{:S(2)}, u32[]{:S(2)}) collective-permute-start(bf16[512,512]{1,0:T(8,128)(2,1)S(1)} %tie.7.nb), channel_id=1, source_target_pairs={{0,1},{1,0},{2,3},{3,2},{4,5},{5,4},{6,7},{7,6},{8,9},{9,8},{10,11... | collective-permute-start | bytes 1572872 | tf_op jit(solution)/shard_map/ppermute | solution.py:434
  47.3 2.6 %collective-permute-start.16 = (bf16[512,512]{1,0:T(8,128)(2,1)S(1)}, bf16[512,512]{1,0:T(8,128)(2,1)S(1)}, u32[]{:S(2)}, u32[]{:S(2)}) collective-permute-start(bf16[512,512]{1,0:T(8,128)(2,1)S(1)} %tie.4.n0), channel_id=1, source_target_pairs={{0,1},{1,0},{2,3},{3,2},{4,5},{5,4},{6,7},{7,6},{8,9},{9,8},{10,11... | collective-permute-start | bytes 1572872 | tf_op jit(solution)/shard_map/ppermute | solution.py:434
  47.8 2.9 %collective-permute-start.17 = (bf16[512,512]{1,0:T(8,128)(2,1)S(1)}, bf16[512,512]{1,0:T(8,128)(2,1)S(1)}, u32[]{:S(2)}, u32[]{:S(2)}) collective-permute-start(bf16[512,512]{1,0:T(8,128)(2,1)S(1)} %tie.6.na), channel_id=1, source_target_pairs={{0,1},{1,0},{2,3},{3,2},{4,5},{5,4},{6,7},{7,6},{8,9},{9,8},{10,11... | collective-permute-start | bytes 1572872 | tf_op jit(solution)/shard_map/ppermute | solution.py:434
  47.9 3.5 %collective-permute-start.19 = (bf16[512,512]{1,0:T(8,128)(2,1)S(1)}, bf16[512,512]{1,0:T(8,128)(2,1)S(1)}, u32[]{:S(2)}, u32[]{:S(2)}) collective-permute-start(bf16[512,512]{1,0:T(8,128)(2,1)S(1)} %collective-permute-done.14.__1_.nc), channel_id=1, source_target_pairs={{0,1},{1,0},{2,3},{3,2},{4,5},{5,4},{6,7},{7,6},{8,9},{9,8},{10,11... | collective-permute-start | bytes 1572872 | tf_op jit(solution)/shard_map/ppermute | solution.py:434
  48.3 16.5 %collective-permute-start.23 = (bf16[512,512]{1,0:T(8,128)(2,1)S(1)}, bf16[512,512]{1,0:T(8,128)(2,1)S(1)}, u32[]{:S(2)}, u32[]{:S(2)}) collective-permute-start(bf16[512,512]{1,0:T(8,128)(2,1)S(1)} %get-tuple-element.59.w_mine), channel_id=1, source_target_pairs={{0,1},{1,0},{2,3},{3,2},{4,5},{5,4},{6,7},{7,6},{8,9},{9,8},{10,11... | collective-permute-start | bytes 1572872 | tf_op jit(solution)/shard_map/ppermute | solution.py:434
  49.2 14.1 %collective-permute-start = (s32[4,128]{1,0:T(4,128)S(1)}, s32[4,128]{1,0:T(4,128)S(1)}, u32[]{:S(2)}, u32[]{:S(2)}) collective-permute-start(s32[4,128]{1,0:T(4,128)S(1)} %pad_add_fusion), channel_id=1, source_target_pairs={{0,0},{1,16},{2,2},{3,18},{4,4},{5,20},{6,6},{7,22},{8,8},{9,24},{... | collective-permute-start | bytes 6152 | tf_op jit(solution)/shard_map/ppermute | solution.py:430
  49.9 19.0 %collective-permute-start.24 = (bf16[512,512]{1,0:T(8,128)(2,1)S(1)}, bf16[512,512]{1,0:T(8,128)(2,1)S(1)}, u32[]{:S(2)}, u32[]{:S(2)}) collective-permute-start(bf16[512,512]{1,0:T(8,128)(2,1)S(1)} %bitcast.23), channel_id=1, source_target_pairs={{0,0},{1,16},{2,2},{3,18},{4,4},{5,20},{6,6},{7,22},{8,8},{9,24},{... | collective-permute-start | bytes 1572872 | tf_op jit(solution)/shard_map/ppermute | solution.py:430
  51.4 13.4 %copy-start.4 = (f32[128]{0:T(128)S(1)}, f32[128]{0:T(128)}, u32[]{:S(2)}) copy-start(f32[128]{0:T(128)} %param.25) | copy-start | bytes 1540
  61.4 7.7 %collective-permute-start.20 = (bf16[528,128]{1,0:T(8,128)(2,1)S(1)}, bf16[528,128]{1,0:T(8,128)(2,1)S(1)}, u32[]{:S(2)}, u32[]{:S(2)}) collective-permute-start(bf16[528,128]{1,0:T(8,128)(2,1)S(1)} %get-tuple-element.56), channel_id=1, source_target_pairs={{0,32},{32,64},{64,96},{96,0},{1,33},{33,65},{65,97},{97,1},{2,34}... | collective-permute-start | bytes 405512 | tf_op jit(solution)/shard_map/ppermute | solution.py:438
  61.9 7.3 %collective-permute-start.21 = (bf16[528,128]{1,0:T(8,128)(2,1)S(1)}, bf16[528,128]{1,0:T(8,128)(2,1)S(1)}, u32[]{:S(2)}, u32[]{:S(2)}) collective-permute-start(bf16[528,128]{1,0:T(8,128)(2,1)S(1)} %get-tuple-element.57), channel_id=1, source_target_pairs={{0,64},{32,96},{64,0},{96,32},{1,65},{33,97},{65,1},{97,33},{2,66}... | collective-permute-start | bytes 405512 | tf_op jit(solution)/shard_map/ppermute | solution.py:438
  63.3 6.8 %collective-permute-start.22 = (bf16[528,128]{1,0:T(8,128)(2,1)S(1)}, bf16[528,128]{1,0:T(8,128)(2,1)S(1)}, u32[]{:S(2)}, u32[]{:S(2)}) collective-permute-start(bf16[528,128]{1,0:T(8,128)(2,1)S(1)} %get-tuple-element.58), channel_id=1, source_target_pairs={{0,96},{32,0},{64,32},{96,64},{1,97},{33,1},{65,33},{97,65},{2,98}... | collective-permute-start | bytes 405512 | tf_op jit(solution)/shard_map/ppermute | solution.py:438
  73.3 15.1 %collective-permute-start.26 = (bf16[512,128]{1,0:T(8,128)(2,1)S(1)}, bf16[512,128]{1,0:T(8,128)(2,1)S(1)}, u32[]{:S(2)}, u32[]{:S(2)}) collective-permute-start(bf16[512,128]{1,0:T(8,128)(2,1)S(1)} %get-tuple-element.81), channel_id=1, source_target_pairs={{0,32},{32,64},{64,96},{96,0},{1,33},{33,65},{65,97},{97,1},{2,34}... | collective-permute-start | bytes 393224 | tf_op jit(solution)/shard_map/ppermute | solution.py:438
  73.9 14.5 %collective-permute-start.27 = (bf16[512,128]{1,0:T(8,128)(2,1)S(1)}, bf16[512,128]{1,0:T(8,128)(2,1)S(1)}, u32[]{:S(2)}, u32[]{:S(2)}) collective-permute-start(bf16[512,128]{1,0:T(8,128)(2,1)S(1)} %get-tuple-element.82), channel_id=1, source_target_pairs={{0,64},{32,96},{64,0},{96,32},{1,65},{33,97},{65,1},{97,33},{2,66}... | collective-permute-start | bytes 393224 | tf_op jit(solution)/shard_map/ppermute | solution.py:438
  77.1 11.3 %collective-permute-start.28 = (bf16[512,128]{1,0:T(8,128)(2,1)S(1)}, bf16[512,128]{1,0:T(8,128)(2,1)S(1)}, u32[]{:S(2)}, u32[]{:S(2)}) collective-permute-start(bf16[512,128]{1,0:T(8,128)(2,1)S(1)} %get-tuple-element.83), channel_id=1, source_target_pairs={{0,96},{32,0},{64,32},{96,64},{1,97},{33,1},{65,33},{97,65},{2,98}... | collective-permute-start | bytes 393224 | tf_op jit(solution)/shard_map/ppermute | solution.py:438
  80.6 27.1 %collective-permute-start.25 = (bf16[512,640]{1,0:T(8,128)(2,1)S(1)}, bf16[512,640]{1,0:T(8,128)(2,1)S(1)}, u32[]{:S(2)}, u32[]{:S(2)}) collective-permute-start(bf16[512,640]{1,0:T(8,128)(2,1)S(1)} %get-tuple-element.76), channel_id=1, source_target_pairs={{0,1},{1,0},{2,3},{3,2},{4,5},{5,4},{6,7},{7,6},{8,9},{9,8},{10,11... | collective-permute-start | bytes 1966088 | tf_op jit(solution)/shard_map/ppermute | solution.py:434
  102.4 5.2 %collective-permute-start.29 = (bf16[512,256]{1,0:T(8,128)(2,1)S(1)}, bf16[512,256]{1,0:T(8,128)(2,1)S(1)}, u32[]{:S(2)}, u32[]{:S(2)}) collective-permute-start(bf16[512,256]{1,0:T(8,128)(2,1)S(1)} %get-tuple-element.93), channel_id=1, source_target_pairs={{0,1},{1,0},{2,3},{3,2},{4,5},{5,4},{6,7},{7,6},{8,9},{9,8},{10,11... | collective-permute-start | bytes 786440 | tf_op jit(solution)/shard_map/ppermute | solution.py:434
  (8 other events, 40.0 us)
